TPU v7x, 32 devices: a whole 2x2x4 slice. The times are simulated.
32 devices in a mesh: clip: 8 (over y, x, core), frame: 4 (over z).
Axes of the slice: x: 2, y: 2, z: 4, core: 2. Of those that a mesh axis runs over, the one named last changes fastest.
Arguments:
- inputs: bfloat16 [16, 16, 256, 768], P('clip', 'frame'), may hold values from -6 to 6
- cotangent: bfloat16 [16, 16, 256, 768], P('clip', 'frame'), may hold values from -6 to 6
- time_steps: int32 [16], P('clip'), may hold values from 0 to 999
- weight_index: int32 [16], P('clip'), may hold values from 0 to 7
- ada_weight: bfloat16 [768, 6912], P(('clip', 'frame')), may hold values from -0.4375 to 0.4375
- ada_bias: bfloat16 [6912], P(('clip', 'frame')), may hold values from -2.390625 to 2.390625
- space_qkv: bfloat16 [768, 2304], P(('clip', 'frame')), may hold values from -0.21875 to 0.21875
- space_out: bfloat16 [768, 768], P(('clip', 'frame')), may hold values from -0.875 to 0.875
- space_out_bias: bfloat16 [768], P(('clip', 'frame')), may hold values from -3 to 3
- time_qkv: bfloat16 [768, 2304], P(('clip', 'frame')), may hold values from -0.21875 to 0.21875
- time_out: bfloat16 [768, 768], P(('clip', 'frame')), may hold values from -0.4375 to 0.4375
- time_out_bias: bfloat16 [768], P(('clip', 'frame')), may hold values from -3 to 3
- up_weight: bfloat16 [768, 3072], P(('clip', 'frame')), may hold values from -0.21875 to 0.21875
- up_bias: bfloat16 [3072], P(('clip', 'frame')), may hold values from -3 to 3
- down_weight: bfloat16 [3072, 768], P(('clip', 'frame')), may hold values from -0.109375 to 0.109375
- down_bias: bfloat16 [768], P(('clip', 'frame')), may hold values from -3 to 3
Outputs:
- block_output: bfloat16 [16, 16, 256, 768], P('clip', 'frame')
- input_grad: float32 [16, 16, 256, 768], P('clip', 'frame')
- grad_ada_weight: float32 [768, 6912], P(('clip', 'frame'))
- grad_ada_bias: float32 [6912], P(('clip', 'frame'))
- grad_space_qkv: float32 [768, 2304], P(('clip', 'frame'))
- grad_space_out: float32 [768, 768], P(('clip', 'frame'))
- grad_space_out_bias: float32 [768], P(('clip', 'frame'))
- grad_time_qkv: float32 [768, 2304], P(('clip', 'frame'))
- grad_time_out: float32 [768, 768], P(('clip', 'frame'))
- grad_time_out_bias: float32 [768], P(('clip', 'frame'))
- grad_up_weight: float32 [768, 3072], P(('clip', 'frame'))
- grad_up_bias: float32 [3072], P(('clip', 'frame'))
- grad_down_weight: float32 [3072, 768], P(('clip', 'frame'))
- grad_down_bias: float32 [768], P(('clip', 'frame'))
All inputs are finite; a program needn't handle non-finite values.
Results may differ from a plain program's by a relative error of at most 0.02.
Values may be sent and summed in bfloat16 or wider, within the bound.
A program may use at most 320 MiB of HBM per device.

v0:
```python
import functools
import math

import jax
import jax.numpy as jnp
from jax import lax
from jax.experimental import pallas as pl
from jax.experimental.pallas import tpu as pltpu
from jax.sharding import PartitionSpec as P

HEADS = 12
HEAD = 64
PAIRS = HEADS // 2
ROWS = 32
GELU_C = math.sqrt(2.0 / math.pi)
GELU_A = 0.044715
VMEM_LIMIT = 58 << 20

f32 = jnp.float32
bf16 = jnp.bfloat16
highest = lax.Precision.HIGHEST
MESH = pl.DeviceIdType.MESH
VMEM = pltpu.VMEM
DMA = pltpu.SemaphoreType.DMA


def embed_steps(time_steps, model_width):
    half_width = model_width // 2
    frequencies = jnp.exp(
        -math.log(10000.0) * jnp.arange(half_width, dtype=f32) / half_width
    )
    angles = time_steps.astype(f32)[:, None] * frequencies[None, :]
    return jnp.concatenate([jnp.cos(angles), jnp.sin(angles)], axis=1)


def dot(left, right, left_dim, right_dim):
    return lax.dot_general(
        left, right, (((left_dim,), (right_dim,)), ((), ())), preferred_element_type=f32
    )


def flip(index, mask):
    bit = 1
    while bit <= mask:
        if mask & bit:
            index = index + bit * (1 - 2 * ((index // bit) % 2))
        bit *= 2
    return index


def span(masks):
    out = [0]
    for mask in masks:
        out = out + [entry ^ mask for entry in out]
    return out


def frame_masks(frames):
    masks, bit = [], 1
    while bit < frames:
        masks.append(bit)
        bit *= 2
    if len(masks) > 1:
        masks = [frames - 1] + masks[:-1]
    return masks


def clip_tail_masks(clips):
    masks, bit = [], 2
    while bit < clips:
        masks.append(bit)
        bit *= 2
    return masks


def greet(clips, frames):
    clip, frame = lax.axis_index("clip"), lax.axis_index("frame")
    barrier = pltpu.get_barrier_semaphore()
    for step in range(1, clips):
        pl.semaphore_signal(
            barrier, inc=1, device_id={"clip": lax.rem(clip + step, clips)}, device_id_type=MESH
        )
    for step in range(1, frames):
        pl.semaphore_signal(
            barrier, inc=1, device_id={"frame": lax.rem(frame + step, frames)}, device_id_type=MESH
        )
    pl.semaphore_wait(barrier, clips + frames - 2)


def spread(axis, size, source_of, target, send_sems, recv_sems):
    me = lax.axis_index(axis)
    copies = []
    for step in range(1, size):
        peer = lax.rem(me + step, size)
        copy = pltpu.make_async_remote_copy(
            src_ref=source_of(peer),
            dst_ref=target.at[me],
            send_sem=send_sems.at[step - 1],
            recv_sem=recv_sems.at[step - 1],
            device_id={axis: peer},
            device_id_type=MESH,
        )
        copy.start()
        copies.append(copy)
    return copies


def start_kernel(
    clips, frames, clip_count,
    x_ref, cotangent, sh_c, sh_b, sh_u, sh_d, embed, select, ada, bias,
    w_c, w_b, w_u, w_d, mod, chosen, totals, hidden_out, qkv_out, mixed_out, branch_out,
    after_first, after_later, cot_first,
    v_c, z_c, z_b, z_u, z_d, st_w, b_c, b_b, b_u, b_d,
    embeds, parts, terms, arrived, held, lined, hidden, qkv, mixed, branch, after,
    zs, zr, cs, cr, xs, xr, ls, es, er, ps, pr, fs, fr, ts, tr, hs, hr, os, ws,
):
    clip, frame = lax.axis_index("clip"), lax.axis_index("frame")
    shards_in = (sh_c, sh_b, sh_u, sh_d)
    zoned = (z_c, z_b, z_u, z_d)
    blocks = (b_c, b_b, b_u, b_d)
    wholes = (v_c, w_b, w_u, w_d)
    width = mod.shape[1]
    frame_count, tokens = x_ref.shape[1], x_ref.shape[2]
    part = tokens // frames
    greet(clips, frames)
    masks = frame_masks(frames)
    sends = []
    stage = {}

    def frame_step(group, step):
        number = (1 << step) - 1
        copies = []
        for offset in span(masks[:step]):
            slot = flip(frame, offset)
            source = shards_in[group] if offset == 0 else zoned[group].at[slot]
            copy = pltpu.make_async_remote_copy(
                src_ref=source,
                dst_ref=zoned[group].at[slot],
                send_sem=zs.at[group, number],
                recv_sem=zr.at[group, number],
                device_id={"frame": flip(frame, masks[step])},
                device_id_type=MESH,
            )
            copy.start()
            copies.append(copy)
            number += 1
        sends.extend(copies)
        stage[group] = copies

    def frame_rest(group):
        for step in range(1, len(masks)):
            for copy in stage[group]:
                copy.wait_recv()
            frame_step(group, step)

    tail = clip_tail_masks(clips)
    steps = len(tail)
    orders = (tail, tail[::-1])
    moving = {}

    def block_send(group, half, step, position, offset):
        whole = wholes[group]
        block_rows = whole.shape[0] // clips
        columns = whole.shape[1] // 2
        rows = pl.ds(pl.multiple_of(flip(clip, offset) * block_rows, block_rows), block_rows)
        lanes = pl.ds(half * columns, columns)
        target = whole.at[rows, lanes]
        number = (1 << step) - 1 + position
        copy = pltpu.make_async_remote_copy(
            src_ref=blocks[group].at[:, lanes] if offset == 0 else target,
            dst_ref=target,
            send_sem=xs.at[group, half, number],
            recv_sem=xr.at[group, half, number],
            device_id={"clip": flip(clip, orders[half][step])},
            device_id_type=MESH,
        )
        copy.start()
        moving[group, half, number] = copy

    core_copies = {group: [] for group in range(4)}

    def core_send(group, offset):
        whole = wholes[group]
        block_rows = whole.shape[0] // clips
        rows = pl.ds(pl.multiple_of(flip(clip, offset) * block_rows, block_rows), block_rows)
        number = len(core_copies[group])
        copy = pltpu.make_async_remote_copy(
            src_ref=blocks[group] if offset == 0 else whole.at[rows, :],
            dst_ref=whole.at[rows, :],
            send_sem=cs.at[group, number],
            recv_sem=cr.at[group, number],
            device_id={"clip": flip(clip, 1)},
            device_id_type=MESH,
        )
        copy.start()
        core_copies[group].append(copy)

    local_copies = []

    def block_ready(group):
        for copy in stage[group]:
            copy.wait_recv()
        rows, columns = shards_in[group].shape
        block_rows = frames * rows
        if rows % 16:
            for slot in range(frames):
                st_w[slot * rows : (slot + 1) * rows, :columns] = zoned[group][slot].astype(f32)
            blocks[group][...] = st_w[:block_rows, :columns].astype(bf16)
        else:
            for slot in range(frames):
                blocks[group][slot * rows : (slot + 1) * rows, :] = zoned[group][slot]
        for step in range(steps):
            for half in range(2):
                block_send(group, half, step, 0, 0)
        core_send(group, 0)
        place = pl.ds(pl.multiple_of(clip * block_rows, block_rows), block_rows)
        keep = pltpu.make_async_copy(blocks[group], wholes[group].at[place, :], ls.at[group])
        keep.start()
        local_copies.append(keep)

    def block_forward(group):
        for step in range(1, steps):
            for half in range(2):
                for position in range(1 << (step - 1), 1 << step):
                    moving[group, half, position - 1].wait_recv()
                for later in range(step, steps):
                    for position, offset in enumerate(span(orders[half][:later])):
                        if (1 << (step - 1)) <= position < (1 << step):
                            block_send(group, half, later, position, offset)

    def block_finish(group):
        last = (1 << (steps - 1)) - 1
        for half in range(2):
            for number in range(last, (1 << steps) - 1):
                moving[group, half, number].wait_recv()
        for offset in span(tail)[1:]:
            core_send(group, offset)

    def core_finish(group):
        for copy in core_copies[group]:
            copy.wait_recv()

    frame_step(0, 0)
    own = spread("clip", clips, lambda peer: embed, embeds, es, er)
    sends.extend(own)
    embeds[clip] = embed[...]
    for group in range(4):
        zoned[group][frame] = shards_in[group][...]
    frame_rest(0)
    for copy in own:
        copy.wait_recv()
    picked = dot(embeds[...].reshape(clips * 16, width), select[...], 1, 0).astype(bf16)
    chosen[...] = picked
    parts[...] = dot(picked, ada[...], 1, 0)
    for peer in range(clips):
        for local in range(clip_count):
            row = peer * 16 + local
            for piece in range(9):
                terms[peer, local * 9 + piece : local * 9 + piece + 1, :] = (
                    parts[row : row + 1, piece * width : (piece + 1) * width]
                    + bias[piece : piece + 1, :]
                )
        base = clip_count * 9
        terms[peer, base : base + 7, :] = bias[9:16, :]
        if base + 7 < ROWS:
            terms[peer, base + 7 : ROWS, :] = jnp.zeros((ROWS - base - 7, width), f32)
    own = spread("clip", clips, lambda peer: terms.at[peer], arrived, ps, pr)
    sends.extend(own)
    arrived[clip] = terms[clip]
    block_ready(0)
    for group in range(1, 4):
        frame_step(group, 0)
    for copy in own:
        copy.wait_recv()
    total = arrived[0]
    for peer in range(1, clips):
        total = total + arrived[peer]
    held[...] = total
    own = spread("frame", frames, lambda peer: held, lined, fs, fr)
    sends.extend(own)
    lined[frame] = total
    for group in range(1, 4):
        frame_rest(group)

    cot_copies = []
    for step in range(1, frames):
        peer = lax.rem(frame + step, frames)
        copy = pltpu.make_async_remote_copy(
            src_ref=cotangent.at[0, :, pl.ds(pl.multiple_of(peer * part, part), part), :],
            dst_ref=cot_first.at[frame],
            send_sem=ts.at[step - 1],
            recv_sem=tr.at[step - 1],
            device_id={"frame": peer},
            device_id_type=MESH,
        )
        copy.start()
        cot_copies.append(copy)
    keep = pltpu.make_async_copy(
        cotangent.at[0, :, pl.ds(pl.multiple_of(frame * part, part), part), :],
        cot_first.at[frame],
        ls.at[4],
    )
    keep.start()
    local_copies.append(keep)

    for copy in own:
        copy.wait_recv()
    total = lined[0]
    for peer in range(1, frames):
        total = total + lined[peer]
    mod[...] = total
    block_forward(0)
    for group in range(1, 4):
        block_ready(group)
    block_finish(0)
    core_finish(0)
    local_copies[0].wait()

    keep = pltpu.make_async_copy(v_c, w_c, ls.at[5])
    keep.start()
    local_copies.append(keep)

    def after_copy(f, step):
        peer = lax.rem(frame + step, frames)
        return pltpu.make_async_remote_copy(
            src_ref=after.at[f, pl.ds(pl.multiple_of(peer * part, part), part), :],
            dst_ref=after_first.at[frame, f],
            send_sem=hs.at[f, step - 1],
            recv_sem=hr.at[f, step - 1],
            device_id={"frame": peer},
            device_id_type=MESH,
        )

    def own_after(f):
        return pltpu.make_async_copy(
            after.at[f, pl.ds(pl.multiple_of(frame * part, part), part), :],
            after_first.at[frame, f],
            os.at[f],
        )

    def later_after(f):
        return pltpu.make_async_copy(after.at[f], after_later.at[f - frame_count], os.at[f])

    kept = ((hidden, hidden_out), (qkv, qkv_out), (mixed, mixed_out), (branch, branch_out))

    def write_back(f):
        return [
            pltpu.make_async_copy(source.at[f], target.at[f], ws.at[number, f])
            for number, (source, target) in enumerate(kept)
        ]

    for local in range(clip_count):
        row = local * 9

        def one_frame(index, carry):
            f = local * frame_count + index
            values = x_ref[local, index].astype(f32)
            norm, _ = normed(values)
            scaled = norm * (1.0 + mod[row + 1 : row + 2, :]) + mod[row : row + 1, :]
            lowered = scaled.astype(bf16)
            hidden[f] = lowered
            qkv[f] = dot(lowered, v_c[:, : 3 * width], 1, 0).astype(bf16)
            attend(qkv.at[f], mixed.at[f], totals.at[f], width, None)
            grown = dot(mixed[f], v_c[:, 3 * width :], 1, 0) + mod[18:19, :]
            branch[f] = grown.astype(bf16)
            after[f] = (values + mod[row + 2 : row + 3, :] * grown).astype(bf16)
            if local == 0:
                for step in range(1, frames):
                    after_copy(f, step).start()
                own_after(f).start()
            else:
                later_after(f).start()
            for copy in write_back(f):
                copy.start()
            return carry

        lax.fori_loop(0, frame_count, one_frame, 0)
        if local == 0:
            block_forward(1)
    for group in range(2, 4):
        block_forward(group)
    for group in range(1, 4):
        block_finish(group)
    for group in range(1, 4):
        core_finish(group)

    def settle(f, carry):
        for step in range(1, frames):
            copy = after_copy(f, step)
            copy.wait_recv()
            copy.wait_send()
        own_after(f).wait()
        return carry

    lax.fori_loop(0, frame_count, settle, 0)

    def settle_later(f, carry):
        later_after(f).wait()
        return carry

    lax.fori_loop(frame_count, clip_count * frame_count, settle_later, 0)

    def settle_kept(f, carry):
        for copy in write_back(f):
            copy.wait()
        return carry

    lax.fori_loop(0, clip_count * frame_count, settle_kept, 0)
    for copy in cot_copies:
        copy.wait_recv()
        copy.wait_send()
    for copy in local_copies[1:]:
        copy.wait()
    for copy in moving.values():
        copy.wait_send()
    for group in range(4):
        for copy in core_copies[group]:
            copy.wait_send()
    for copy in sends:
        copy.wait_send()


def start_call(
    clips, frames, inputs, cotangent, sh_c, sh_b, sh_u, sh_d, embed, select, ada, bias
):
    clip_count, frame_count, tokens, width = inputs.shape
    rows, columns = sh_c.shape
    rows_d = sh_d.shape[0]
    block = frames * rows
    block_d = frames * rows_d
    peers = max(clips // 2 - 1, 1)
    total = clip_count * frame_count
    part = tokens // frames
    whole = jax.ShapeDtypeStruct((clips * block, columns), bf16)
    vmem = pl.BlockSpec(memory_space=VMEM)
    hbm = pl.BlockSpec(memory_space=pl.ANY)
    zoned = lambda height, lanes: VMEM((frames, height, lanes), bf16)
    saved = lambda lanes: jax.ShapeDtypeStruct((total, tokens, lanes), bf16)
    lent = lambda lanes: VMEM((total, tokens, lanes), bf16)
    traded = jax.ShapeDtypeStruct((frames, frame_count, part, width), bf16)
    return pl.pallas_call(
        functools.partial(start_kernel, clips, frames, clip_count),
        out_shape=(
            whole, whole, whole,
            jax.ShapeDtypeStruct((clips * block_d, width), bf16),
            jax.ShapeDtypeStruct((ROWS, width), f32),
            jax.ShapeDtypeStruct((clips * 16, 128), bf16),
            jax.ShapeDtypeStruct((total, 16, tokens), f32),
            saved(width), saved(3 * width), saved(width), saved(width),
            traded,
            jax.ShapeDtypeStruct(((clip_count - 1) * frame_count, tokens, width), bf16),
            traded,
        ),
        in_specs=[vmem, hbm] + [vmem] * 8,
        out_specs=(hbm, hbm, hbm, hbm, vmem, vmem, vmem) + (hbm,) * 7,
        scratch_shapes=[
            VMEM((clips * block, columns), bf16),
            zoned(rows, columns), zoned(rows, columns), zoned(rows, columns), zoned(rows_d, width),
            VMEM((max(block, block_d), columns), f32),
            VMEM((block, columns), bf16),
            VMEM((block, columns), bf16),
            VMEM((block, columns), bf16),
            VMEM((block_d, width), bf16),
            VMEM((clips, 16, width), bf16),
            VMEM((clips * 16, 9 * width), f32),
            VMEM((clips, ROWS, width), f32),
            VMEM((clips, ROWS, width), f32),
            VMEM((ROWS, width), f32),
            VMEM((frames, ROWS, width), f32),
            lent(width), lent(3 * width), lent(width), lent(width), lent(width),
            DMA((4, frames - 1)), DMA((4, frames - 1)),
            DMA((4, clips // 2)), DMA((4, clips // 2)),
            DMA((4, 2, peers)), DMA((4, 2, peers)),
            DMA((6,)),
            DMA((clips - 1,)), DMA((clips - 1,)),
            DMA((clips - 1,)), DMA((clips - 1,)),
            DMA((frames - 1,)), DMA((frames - 1,)),
            DMA((frames - 1,)), DMA((frames - 1,)),
            DMA((frame_count, frames - 1)), DMA((frame_count, frames - 1)),
            DMA((total,)),
            DMA((4, total)),
        ],
        compiler_params=pltpu.CompilerParams(
            collective_id=0, has_side_effects=True, vmem_limit_bytes=VMEM_LIMIT
        ),
    )(inputs, cotangent, sh_c, sh_b, sh_u, sh_d, embed, select, ada, bias)


STEP = 512
SLOTS = 3


def grad_kernel(
    clips, frames, clip_count,
    small, chosen, out_all, h3, gup, act, gb3, h2, gqkv2, mix2, gb2, h1, gqkv1, mix1, gb1,
    outputs, grad_ada, bias_sums, out_u, out_d, out_b, out_bo, out_c, out_co,
    sum_w, sum_d, core_w, core_d, side_w, side_d, line_w, line_d, last_w, last_d,
    left, right, total, gathered, lined, held,
    lsem, rsem, cs, cr, xs, xr, zs, zr, fs, fr, ps, pr, os, orr, ks,
):
    clip, frame = lax.axis_index("clip"), lax.axis_index("frame")
    tokens = h3.shape[0]
    width = small.shape[1]
    wide = sum_w.shape[-1]
    narrow = sum_d.shape[-1]
    tail = clip_tail_masks(clips)
    orders = (tail, tail[::-1])
    masks = frame_masks(frames)
    greet(clips, frames)
    first = spread("frame", frames, lambda peer: small, lined, fs, fr)
    lined[frame] = small[...]
    part = out_all.shape[3]
    frame_count = out_all.shape[2]
    out_copies = []
    mine = pl.ds(pl.multiple_of(frame * part, part), part)

    def send_output(number):
        local, index = divmod(number, frame_count)
        for hop in range(1, frames):
            peer = lax.rem(frame + hop, frames)
            copy = pltpu.make_async_remote_copy(
                src_ref=out_all.at[local, peer, index],
                dst_ref=outputs.at[local, index, mine, :],
                send_sem=os.at[number, hop - 1],
                recv_sem=orr.at[number, hop - 1],
                device_id={"frame": peer},
                device_id_type=MESH,
            )
            copy.start()
            out_copies.append(copy)

    own_outs = []
    for local in range(clip_count):
        copy = pltpu.make_async_copy(
            out_all.at[local, frame], outputs.at[local, :, mine, :], ks.at[local]
        )
        copy.start()
        own_outs.append(copy)

    chunks = [
        (1, 0, [(act, gb3, 0, 0, narrow)], out_d, 0),
        (1, 1, [(act, gb3, narrow, 0, narrow)], out_d, narrow),
        (0, 0, [(h3, gup, 0, 0, wide)], out_u, 0),
        (0, 1, [(h3, gup, wide, 0, wide)], out_u, wide),
        (0, 2, [(h2, gqkv2, 0, 0, wide)], out_b, 0),
        (0, 3, [(h2, gqkv2, wide, 0, width), (mix2, gb2, 0, width, width)], out_b, wide),
        (0, 4, [(h1, gqkv1, 0, 0, wide)], out_c, 0),
        (0, 5, [(h1, gqkv1, wide, 0, width), (mix1, gb1, 0, width, width)], out_c, wide),
    ]
    sums, cores, sides = (sum_w, sum_d), (core_w, core_d), (side_w, side_d)
    lines, lasts = (line_w, line_d), (last_w, last_d)
    flights = {}

    steps = tokens // STEP
    line_up = []
    for kind, _, parts, _, _ in chunks:
        for part in parts:
            for group in range(part[0].shape[1] // width):
                line_up.append(part[:3] + (part[3] + group * part[4], part[4], group))
    begins = [0]
    for kind, _, parts, _, _ in chunks:
        begins.append(begins[-1] + sum(part[0].shape[1] // width for part in parts))

    def load(entry, step, slot):
        one, other, begin, _, lanes, group = line_up[entry]
        rows = pl.ds(pl.multiple_of(step * STEP, STEP), STEP)
        return (
            pltpu.make_async_copy(
                one.at[rows, pl.ds(group * width, width)], left.at[slot], lsem.at[slot]
            ),
            pltpu.make_async_copy(
                other.at[rows, pl.ds(begin, lanes)],
                right.at[slot, :, pl.ds(0, lanes)],
                rsem.at[slot],
            ),
        )

    def place_of(entry, step):
        return lax.rem(entry * steps + step, SLOTS)

    def multiply(number):
        kind, place = chunks[number][:2]
        for entry in range(begins[number], begins[number + 1]):
            at, lanes = line_up[entry][3:5]

            def body(step, carry):
                ahead = step + SLOTS - 1

                @pl.when(ahead < steps)
                def _():
                    for copy in load(entry, ahead, place_of(entry, ahead)):
                        copy.start()

                if entry + 1 < len(line_up):

                    @pl.when(ahead >= steps)
                    def _():
                        for copy in load(entry + 1, ahead - steps, place_of(entry, ahead)):
                            copy.start()

                slot = place_of(entry, step)
                for copy in load(entry, step, slot):
                    copy.wait()
                columns = slice(at, at + lanes)
                before = jnp.where(step > 0, total[:, columns], 0.0)
                total[:, columns] = before + dot(left[slot], right[slot, :, :lanes], 0, 0)
                return carry

            lax.fori_loop(0, steps, body, 0)
        rows, lanes = sums[kind].shape[2:]
        for block in range(clips):
            begin = block * rows
            column = begin // width * lanes
            begin = begin % width
            sums[kind][place, block] = total[begin : begin + rows, column : column + lanes].astype(
                bf16
            )

    def core_start(number):
        kind, place = chunks[number][:2]
        copies = []
        for position, offset in enumerate(span(tail)):
            copy = pltpu.make_async_remote_copy(
                src_ref=sums[kind].at[place, flip(clip, offset ^ 1)],
                dst_ref=cores[kind].at[place, position],
                send_sem=cs.at[number, position],
                recv_sem=cr.at[number, position],
                device_id={"clip": flip(clip, 1)},
                device_id_type=MESH,
            )
            copy.start()
            copies.append(copy)
        flights[number, "core"] = copies

    def half_of(kind, half):
        if kind:
            rows = sums[kind].shape[2] // 2
            return (slice(half * rows, (half + 1) * rows), slice(None))
        lanes = sums[kind].shape[3] // 2
        return (slice(None), slice(half * lanes, (half + 1) * lanes))

    def side_start(number, step):
        kind, place = chunks[number][:2]
        copies = []
        for half in range(2):
            mask = orders[half][step]
            for position, offset in enumerate(span(orders[half][:step])):
                entry = (1 << step) - 1 + position
                copy = pltpu.make_async_remote_copy(
                    src_ref=sums[kind].at[(place, flip(clip, offset ^ mask)) + half_of(kind, half)],
                    dst_ref=sides[kind].at[place, half, entry],
                    send_sem=xs.at[number, half, entry],
                    recv_sem=xr.at[number, half, entry],
                    device_id={"clip": flip(clip, mask)},
                    device_id_type=MESH,
                )
                copy.start()
                copies.append(copy)
        flights[number, "side", step] = copies

    def core_add(number):
        kind, place = chunks[number][:2]
        for copy in flights[number, "core"]:
            copy.wait_recv()
        for position, offset in enumerate(span(tail)):
            block = flip(clip, offset)
            sums[kind][place, block] = (
                sums[kind][place, block].astype(f32) + cores[kind][place, position].astype(f32)
            ).astype(bf16)
        side_start(number, len(tail) - 1)

    def side_add(number, step):
        kind, place = chunks[number][:2]
        for copy in flights[number, "side", step]:
            copy.wait_recv()
        for half in range(2):
            for position, offset in enumerate(span(orders[half][:step])):
                entry = (1 << step) - 1 + position
                block = flip(clip, offset)
                where = (place, block) + half_of(kind, half)
                sums[kind][where] = (
                    sums[kind][where].astype(f32) + sides[kind][place, half, entry].astype(f32)
                ).astype(bf16)
        if step:
            side_start(number, step - 1)
        else:
            rows = lines[kind].shape[2]
            block = sums[kind][place, clip].astype(f32)
            for slot in range(frames):
                lines[kind][place, slot] = block[slot * rows : (slot + 1) * rows, :].astype(bf16)
            line_start(number, len(masks) - 1)

    def line_start(number, step):
        kind, place = chunks[number][:2]
        copies = []
        for position, offset in enumerate(span(masks[:step])):
            entry = (1 << step) - 1 + position
            copy = pltpu.make_async_remote_copy(
                src_ref=lines[kind].at[place, flip(frame, offset ^ masks[step])],
                dst_ref=lasts[kind].at[place, entry],
                send_sem=zs.at[number, entry],
                recv_sem=zr.at[number, entry],
                device_id={"frame": flip(frame, masks[step])},
                device_id_type=MESH,
            )
            copy.start()
            copies.append(copy)
        flights[number, "line", step] = copies

    def line_add(number, step):
        kind, place, _, target, begin = chunks[number]
        for copy in flights[number, "line", step]:
            copy.wait_recv()
        for position, offset in enumerate(span(masks[:step])):
            entry = (1 << step) - 1 + position
            slot = flip(frame, offset)
            value = lines[kind][place, slot].astype(f32) + lasts[kind][place, entry].astype(f32)
            if step:
                lines[kind][place, slot] = value.astype(bf16)
            elif begin + value.shape[1] > target.shape[1]:
                cut = target.shape[1] - begin
                target[:, begin:] = value[:, :cut]
                (out_bo if target is out_b else out_co)[...] = value[:, cut:]
            else:
                target[:, begin : begin + value.shape[1]] = value
        if step:
            line_start(number, step - 1)

    stages = [core_start, core_add]
    for step in range(len(tail))[::-1]:
        stages.append(functools.partial(side_add, step=step))
    for step in range(len(masks))[::-1]:
        stages.append(functools.partial(line_add, step=step))

    def finish_small():
        for copy in second:
            copy.wait_recv()
        rows = grad_ada.shape[0]
        for number in range(9):
            terms = [
                gathered[peer, local * 9 + number : local * 9 + number + 1, :]
                for peer in range(clips)
                for local in range(clip_count)
            ]
            terms = jnp.concatenate(terms, axis=0)
            grad_ada[:, number * width : (number + 1) * width] = lax.dot_general(
                chosen[...], terms, (((1,), (0,)), ((), ())), precision=highest,
                preferred_element_type=f32,
            )[:rows, :]
            bias_sums[number : number + 1, :] = column_sum(terms)
        base = clip_count * 9
        summed = gathered[0, base : base + 7, :]
        for peer in range(1, clips):
            summed = summed + gathered[peer, base : base + 7, :]
        bias_sums[9:16, :] = summed

    for step in range(SLOTS - 1):
        for copy in load(0, step, step):
            copy.start()
    second = None
    lags = [0, 1, 3]
    while len(lags) < len(stages):
        lags.append(lags[-1] + 1)
    for turn in range(len(chunks) + lags[-1]):
        for depth in range(len(stages))[::-1]:
            if depth > 0 and 0 <= turn - lags[depth] < len(chunks):
                stages[depth](turn - lags[depth])
        if turn < clip_count * frame_count:
            send_output(turn)
        if turn < len(chunks):
            multiply(turn)
            core_start(turn)
        if turn == len(chunks):
            finish_small()
        if turn == 0:
            for copy in first:
                copy.wait_recv()
            summed = lined[0]
            for peer in range(1, frames):
                summed = summed + lined[peer]
            held[...] = summed
            second = spread("clip", clips, lambda peer: held, gathered, ps, pr)
            gathered[clip] = summed
    for copy in own_outs:
        copy.wait()
    for copy in out_copies:
        copy.wait_recv()
        copy.wait_send()
    for copy in first + second:
        copy.wait_send()
    for copies in flights.values():
        for copy in copies:
            copy.wait_send()


def grad_call(clips, frames, clip_count, small, chosen, out_all, *operands):
    h3, gup, act = operands[:3]
    _, _, frame_count, part, _ = out_all.shape
    width, hidden = h3.shape[1], act.shape[1]
    owners = clips * frames
    wide, narrow = hidden // 2, width // 2
    rows_w, rows_d = width // owners, hidden // owners
    peers = max(clips // 2 - 1, 1)
    vmem = pl.BlockSpec(memory_space=VMEM)
    hbm = pl.BlockSpec(memory_space=pl.ANY)

    return pl.pallas_call(
        functools.partial(grad_kernel, clips, frames, clip_count),
        out_shape=(
            jax.ShapeDtypeStruct((clip_count, frame_count, frames * part, width), bf16),
            jax.ShapeDtypeStruct((rows_w, 9 * width), f32),
            jax.ShapeDtypeStruct((16, width), f32),
            jax.ShapeDtypeStruct((rows_w, hidden), f32),
            jax.ShapeDtypeStruct((rows_d, width), f32),
            jax.ShapeDtypeStruct((rows_w, 3 * width), f32),
            jax.ShapeDtypeStruct((rows_w, width), f32),
            jax.ShapeDtypeStruct((rows_w, 3 * width), f32),
            jax.ShapeDtypeStruct((rows_w, width), f32),
        ),
        in_specs=[vmem, vmem] + [hbm] * (1 + len(operands)),
        out_specs=(hbm,) + (vmem,) * 8,
        scratch_shapes=[
            VMEM((6, clips, rows_w * frames, wide), bf16),
            VMEM((2, clips, rows_d * frames, narrow), bf16),
            VMEM((6, clips // 2, rows_w * frames, wide), bf16),
            VMEM((2, clips // 2, rows_d * frames, narrow), bf16),
            VMEM((6, 2, peers, rows_w * frames, wide // 2), bf16),
            VMEM((2, 2, peers, rows_d * frames // 2, narrow), bf16),
            VMEM((6, frames, rows_w, wide), bf16),
            VMEM((2, frames, rows_d, narrow), bf16),
            VMEM((6, frames - 1, rows_w, wide), bf16),
            VMEM((2, frames - 1, rows_d, narrow), bf16),
            VMEM((SLOTS, STEP, width), bf16),
            VMEM((SLOTS, STEP, wide), bf16),
            VMEM((width, wide), f32),
            VMEM((clips,) + small.shape, f32),
            VMEM((frames,) + small.shape, f32),
            VMEM(small.shape, f32),
            DMA((SLOTS,)), DMA((SLOTS,)),
            DMA((8, clips // 2)), DMA((8, clips // 2)),
            DMA((8, 2, peers)), DMA((8, 2, peers)),
            DMA((8, frames - 1)), DMA((8, frames - 1)),
            DMA((frames - 1,)), DMA((frames - 1,)),
            DMA((clips - 1,)), DMA((clips - 1,)),
            DMA((clip_count * frame_count, frames - 1)),
            DMA((clip_count * frame_count, frames - 1)),
            DMA((clip_count,)),
        ],
        compiler_params=pltpu.CompilerParams(
            collective_id=1, has_side_effects=True, vmem_limit_bytes=VMEM_LIMIT
        ),
    )(small, chosen, out_all, *operands)


def normed(values):
    centred = values - jnp.mean(values, axis=-1, keepdims=True)
    scale = lax.rsqrt(jnp.mean(centred * centred, axis=-1, keepdims=True) + 1e-06)
    return centred * scale, scale


def norm_back(grad, scaled, norm, scale):
    inner = grad * scaled
    return scale * (
        inner
        - jnp.mean(inner, axis=-1, keepdims=True)
        - norm * jnp.mean(inner * norm, axis=-1, keepdims=True)
    )


def column_sum(values):
    return jnp.sum(values, axis=0, keepdims=True)


def attend(qkv, mixed, totals, width, mask):
    tokens = qkv.shape[0]
    low = lax.broadcasted_iota(jnp.int32, (tokens, 128), 1) < HEAD
    for pair in range(PAIRS):
        at = pair * 128
        queries = qkv[:, at : at + 128] * bf16(0.125)
        keys = qkv[:, width + at : width + at + 128]
        values = qkv[:, 2 * width + at : 2 * width + at + 128]
        halves = []
        for half in range(2):
            own = jnp.where(low if half == 0 else ~low, queries, bf16(0))
            scores = dot(keys, own, 1, 1)
            if mask is not None:
                scores = scores + mask[...]
            peak = jnp.max(scores, axis=0, keepdims=True)
            terms = jnp.exp(scores - peak)
            total = jnp.sum(terms, axis=0, keepdims=True)
            weights = (terms * (1.0 / total)).astype(bf16)
            totals[2 * pair + half : 2 * pair + half + 1, :] = peak + jnp.log(total)
            halves.append(dot(weights, values, 0, 0))
        mixed[:, at : at + 128] = jnp.where(low, halves[0], halves[1]).astype(bf16)


def attend_back(qkv, grad_mixed, totals, grad_qkv, width, mask):
    tokens = qkv.shape[0]
    low = lax.broadcasted_iota(jnp.int32, (tokens, 128), 1) < HEAD
    for pair in range(PAIRS):
        at = pair * 128
        queries = qkv[:, at : at + 128]
        keys = qkv[:, width + at : width + at + 128]
        values = qkv[:, 2 * width + at : 2 * width + at + 128]
        grads = grad_mixed[:, at : at + 128]
        halves = []
        for half in range(2):
            pick = low if half == 0 else ~low
            own = jnp.where(pick, queries * bf16(0.125), bf16(0))
            own_grads = jnp.where(pick, grads, bf16(0))
            scores = dot(keys, own, 1, 1)
            if mask is not None:
                scores = scores + mask[...]
            weights = jnp.exp(scores - totals[2 * pair + half : 2 * pair + half + 1, :])
            grad_weights = dot(values, own_grads, 1, 1)
            inner = jnp.sum(weights * grad_weights, axis=0, keepdims=True)
            grad_scores = (weights * (grad_weights - inner)).astype(bf16)
            halves.append(
                (
                    dot(grad_scores, keys, 0, 0),
                    dot(grad_scores, queries, 1, 0),
                    dot(weights.astype(bf16), grads, 1, 0),
                )
            )
        for part, factor in ((0, 0.125), (1, 0.125), (2, 1.0)):
            joined = jnp.where(low, halves[0][part], halves[1][part]) * factor
            start = part * width + at
            grad_qkv[:, start : start + 128] = joined.astype(bf16)


def full(shape):
    return pl.BlockSpec(shape, lambda *_: (0,) * len(shape), pipeline_mode=pl.Buffered(1))


def middle_kernel(
    clips, frames, tiles,
    after_first, cot_first, after_later, cotangent, loss, mod, w_b, w_u, w_d,
    act_ref, gup_ref, h3_ref, gb3_ref, mixed_ref, gb2_ref, h2_ref, gqkv_ref, sums,
    after_second, cot_second, grad_first, grad_later, out_all,
    qkv, totals, mask, gmix, after_tile, cot_tile, grad_stage, out_stage,
    ts, tr, us, ur, gs, gr, ls, ks, ws,
):
    frame = lax.axis_index("frame")
    step = pl.program_id(0)
    last = pl.num_programs(0) - 1
    clip = lax.div(step, tiles)
    tile = lax.rem(step, tiles)
    slot = lax.rem(step, 2)
    width = mod.shape[1]
    frame_count, group = after_tile.shape[2], after_tile.shape[3]
    part = tiles * group
    tokens = frames * frame_count * group
    row = clip * 9
    piece = lambda number: mod[pl.ds(row + number, 1), :]

    def own_part(index):
        return pl.ds(pl.multiple_of(index * part, part), part)

    def later_copies(number):
        copies = []
        for hop in range(1, frames):
            peer = lax.rem(frame + hop, frames)
            if number:
                source, target, send, recv = cotangent.at[1, :, own_part(peer), :], cot_second, us, ur
            else:
                source, target, send, recv = after_later.at[:, own_part(peer), :], after_second, ts, tr
            copies.append(
                pltpu.make_async_remote_copy(
                    src_ref=source,
                    dst_ref=target.at[frame],
                    send_sem=send.at[hop - 1],
                    recv_sem=recv.at[hop - 1],
                    device_id={"frame": peer},
                    device_id_type=MESH,
                )
            )
        return copies

    def own_copy(number):
        source = cotangent.at[1] if number else after_later
        target = cot_second if number else after_second
        return pltpu.make_async_copy(
            source.at[:, own_part(frame), :], target.at[frame], ks.at[number]
        )

    def load(source, number, index, place):
        rows = pl.ds(pl.multiple_of(index * group, group), group)
        target = (after_tile, cot_tile)[number].at[place]
        return pltpu.make_async_copy(source.at[:, :, rows, :], target, ls.at[place, number])

    def grad_copies(index):
        rows = pl.ds(pl.multiple_of(index * group, group), group)
        copies = []
        for hop in range(1, frames):
            peer = lax.rem(frame + hop, frames)
            copies.append(
                pltpu.make_async_remote_copy(
                    src_ref=grad_stage.at[index, peer],
                    dst_ref=grad_first.at[frame, :, rows, :],
                    send_sem=gs.at[index, hop - 1],
                    recv_sem=gr.at[index, hop - 1],
                    device_id={"frame": peer},
                    device_id_type=MESH,
                )
            )
        return copies

    def grad_own(index):
        rows = pl.ds(pl.multiple_of(index * group, group), group)
        return pltpu.make_async_copy(
            grad_stage.at[index, frame], grad_first.at[frame, :, rows, :], ws.at[0, index]
        )

    def grad_keep(index):
        place = index + tiles
        rows = pl.ds(pl.multiple_of(index * group, group), group)
        return pltpu.make_async_copy(
            grad_stage.at[place], grad_later.at[:, :, rows, :], ws.at[0, place]
        )

    def out_keep(number):
        rows = pl.ds(pl.multiple_of(lax.rem(number, tiles) * group, group), group)
        return pltpu.make_async_copy(
            out_stage.at[number], out_all.at[lax.div(number, tiles), :, :, rows, :], ws.at[1, number]
        )

    @pl.when(step == 0)
    def _():
        barrier = pltpu.get_barrier_semaphore()
        for hop in range(1, frames):
            pl.semaphore_signal(
                barrier,
                inc=1,
                device_id={"frame": lax.rem(frame + hop, frames)},
                device_id_type=MESH,
            )
        pl.semaphore_wait(barrier, frames - 1)
        load(after_first, 0, 0, 0).start()
        load(cot_first, 1, 0, 0).start()
        for number in range(2):
            for copy in later_copies(number):
                copy.start()
            own_copy(number).start()
        first = lax.broadcasted_iota(jnp.int32, (tokens, tokens), 0)
        second = lax.broadcasted_iota(jnp.int32, (tokens, tokens), 1)
        mask[...] = jnp.where(lax.rem(first, group) == lax.rem(second, group), 0.0, -1e30)

    @pl.when(step == tiles)
    def _():
        for copy in later_copies(0):
            copy.wait_recv()
        own_copy(0).wait()
        load(after_second, 0, 0, slot).start()

    load(after_first, 0, 0, slot).wait()

    @pl.when(step + 1 < tiles)
    def _():
        load(after_first, 0, step + 1, 1 - slot).start()
        load(cot_first, 1, step + 1, 1 - slot).start()

    @pl.when((step >= tiles) & (step < last))
    def _():
        load(after_second, 0, tile + 1, 1 - slot).start()

    @pl.when((step > tiles) & (step < last))
    def _():
        load(cot_second, 1, tile + 1, 1 - slot).start()

    @pl.when(tile == 0)
    def _():
        sums[...] = jnp.zeros_like(sums)

    def add(place, values):
        sums[place : place + 1, :] += values

    after = after_tile[slot].reshape(tokens, width).astype(f32)
    norm, scale = normed(after)
    hidden = (norm * (1.0 + piece(4)) + piece(3)).astype(bf16)
    h2_ref[...] = hidden
    qkv[...] = dot(hidden, w_b[:, : 3 * width], 1, 0).astype(bf16)
    attend(qkv, mixed_ref, totals, width, mask)
    branch_two = dot(mixed_ref[...], w_b[:, 3 * width :], 1, 0) + mod[19:20, :]
    after_two = after + piece(5) * branch_two
    norm_three, scale_three = normed(after_two)
    hidden = (norm_three * (1.0 + piece(7)) + piece(6)).astype(bf16)
    h3_ref[...] = hidden

    @pl.when(step == tiles)
    def _():
        for copy in later_copies(1):
            copy.wait_recv()
        own_copy(1).wait()
        load(cot_second, 1, 0, slot).start()
        if tiles > 1:
            load(cot_second, 1, 1, 1 - slot).start()

        def send(index, carry):
            for copy in grad_copies(index):
                copy.start()
            return carry

        lax.fori_loop(0, tiles, send, 0)

    load(cot_first, 1, 0, slot).wait()
    grad_out = cot_tile[slot].reshape(tokens, width).astype(f32) * loss[pl.ds(clip, 1), :]
    grad_branch = (grad_out * piece(8)).astype(bf16)
    gb3_ref[...] = grad_branch
    add(11, column_sum(grad_branch.astype(f32)))
    branch_three = jnp.zeros((tokens, width), f32)
    grad_hidden = jnp.zeros((tokens, width), f32)
    for chunk in range(w_u.shape[1] // width):
        cut = slice(chunk * width, (chunk + 1) * width)
        upper = dot(hidden, w_u[:, cut], 1, 0) + mod[20 + chunk : 21 + chunk, :]
        square = upper * upper
        bend = jnp.tanh(upper * (GELU_C + (GELU_C * GELU_A) * square))
        half = 0.5 + 0.5 * bend
        act = (upper * half).astype(bf16)
        slope = half + (0.5 * upper) * (1.0 - bend * bend) * (
            GELU_C + (3.0 * GELU_C * GELU_A) * square
        )
        act_ref[:, cut] = act
        branch_three += dot(act, w_d[cut, :], 1, 0)
        grad_upper = (dot(grad_branch, w_d[cut, :], 1, 1) * slope).astype(bf16)
        gup_ref[:, cut] = grad_upper
        add(7 + chunk, column_sum(grad_upper.astype(f32)))
        grad_hidden += dot(grad_upper, w_u[:, cut], 1, 1)
    branch_three += mod[24:25, :]
    out = (after_two + piece(8) * branch_three).astype(bf16)
    out_stage[step] = out.reshape(out_stage.shape[1:])
    add(5, column_sum(grad_out * branch_three))
    add(3, column_sum(grad_hidden))
    add(4, column_sum(grad_hidden * norm_three))
    grad_two = grad_out + norm_back(grad_hidden, 1.0 + piece(7), norm_three, scale_three)
    add(2, column_sum(grad_two * branch_two))
    grad_branch = (grad_two * piece(5)).astype(bf16)
    gb2_ref[...] = grad_branch
    add(6, column_sum(grad_branch.astype(f32)))
    gmix[...] = dot(grad_branch, w_b[:, 3 * width :], 1, 1).astype(bf16)
    attend_back(qkv, gmix, totals, gqkv_ref, width, mask)
    grad_hidden = dot(gqkv_ref[...], w_b[:, : 3 * width], 1, 1).astype(bf16).astype(f32)
    add(0, column_sum(grad_hidden))
    add(1, column_sum(grad_hidden * norm))
    grad_one = grad_two + norm_back(grad_hidden, 1.0 + piece(4), norm, scale)
    grad_stage[step] = grad_one.astype(bf16).reshape(grad_stage.shape[1:])

    out_keep(step).start()

    @pl.when(step < tiles)
    def _():
        grad_own(tile).start()

    @pl.when(step >= tiles)
    def _():
        grad_keep(tile).start()

    @pl.when(step == last)
    def _():
        for copy in later_copies(0) + later_copies(1):
            copy.wait_send()

        def settle(index, carry):
            for copy in grad_copies(index):
                copy.wait_send()
                copy.wait_recv()
            grad_own(index).wait()
            grad_keep(index).wait()
            out_keep(index).wait()
            out_keep(index + tiles).wait()
            return carry

        lax.fori_loop(0, tiles, settle, 0)


def middle_call(
    clips, frames, after_first, cot_first, after_later, cotangent, loss, mod, w_b, w_u, w_d
):
    _, frame_count, part, width = after_first.shape
    group = min(16, part)
    tiles = part // group
    tokens = frames * frame_count * group
    hidden_width = w_u.shape[1]
    widths = (hidden_width, hidden_width, width, width, width, width, width, 3 * width)
    own = lambda columns: pl.BlockSpec((tokens, columns), lambda t: (t, 0))
    hbm = pl.BlockSpec(memory_space=pl.ANY)
    rows = 2 * tiles * tokens
    traded = jax.ShapeDtypeStruct(after_first.shape, bf16)
    slab = (frames, frame_count, group, width)
    return pl.pallas_call(
        functools.partial(middle_kernel, clips, frames, tiles),
        grid=(2 * tiles,),
        in_specs=[
            hbm, hbm, hbm, hbm, full(loss.shape), full(mod.shape), full(w_b.shape),
            full(w_u.shape), full(w_d.shape),
        ],
        out_specs=[own(columns) for columns in widths]
        + [pl.BlockSpec((None, 16, width), lambda t: (t // tiles, 0, 0))]
        + [hbm] * 5,
        out_shape=[jax.ShapeDtypeStruct((rows, columns), bf16) for columns in widths]
        + [
            jax.ShapeDtypeStruct((2, 16, width), f32),
            traded, traded, traded, traded,
            jax.ShapeDtypeStruct((2,) + after_first.shape, bf16),
        ],
        scratch_shapes=[
            VMEM((tokens, 3 * width), bf16),
            VMEM((16, tokens), f32),
            VMEM((tokens, tokens), f32),
            VMEM((tokens, width), bf16),
            VMEM((2,) + slab, bf16),
            VMEM((2,) + slab, bf16),
            VMEM((2 * tiles,) + slab, bf16),
            VMEM((2 * tiles,) + slab, bf16),
            DMA((frames - 1,)), DMA((frames - 1,)),
            DMA((frames - 1,)), DMA((frames - 1,)),
            DMA((tiles, frames - 1)), DMA((tiles, frames - 1)),
            DMA((2, 2)), DMA((2,)), DMA((2, 2 * tiles)),
        ],
        compiler_params=pltpu.CompilerParams(
            collective_id=2, has_side_effects=True, vmem_limit_bytes=VMEM_LIMIT
        ),
    )(after_first, cot_first, after_later, cotangent, loss, mod, w_b, w_u, w_d)


def space_back_kernel(
    clip, grad_ref, x_ref, mod, w_c, qkv, branch, totals,
    out_ref, gb_ref, gqkv_ref, sums, gmix,
):
    width = x_ref.shape[-1]
    tokens = x_ref.shape[-2]
    row = clip * 9
    piece = lambda number: mod[row + number : row + number + 1, :]

    @pl.when(pl.program_id(0) == 0)
    def _():
        sums[...] = jnp.zeros_like(sums)

    grad = grad_ref[...].reshape(tokens, width).astype(f32)
    grad_branch = (grad * piece(2)).astype(bf16)
    gb_ref[...] = grad_branch
    sums[2:3, :] += column_sum(grad * branch[...].astype(f32))
    sums[3:4, :] += column_sum(grad_branch.astype(f32))
    gmix[...] = dot(grad_branch, w_c[:, 3 * width :], 1, 1).astype(bf16)
    attend_back(qkv, gmix, totals, gqkv_ref, width, None)
    grad_hidden = dot(gqkv_ref[...], w_c[:, : 3 * width], 1, 1)
    norm, scale = normed(x_ref[...].reshape(tokens, width).astype(f32))
    sums[0:1, :] += column_sum(grad_hidden)
    sums[1:2, :] += column_sum(grad_hidden * norm)
    result = grad + norm_back(grad_hidden, 1.0 + piece(1), norm, scale)
    out_ref[...] = result.reshape(out_ref.shape)


def space_back_next(count, clip, *refs):
    space_back_kernel(clip, *refs[:7], *refs[7 + count :])


def space_back_call(clip, grad, x, mod, w_c, qkv, branch, totals, earlier):
    clip_count, frame_count, tokens, width = x.shape
    frames = grad.shape[0]
    part = grad.shape[2]
    rows = frame_count * tokens
    by_frame = lambda columns: pl.BlockSpec(
        (None, tokens, columns), lambda f: (clip * frame_count + f, 0, 0)
    )
    own = lambda columns: pl.BlockSpec((tokens, columns), lambda f: (clip * frame_count + f, 0))
    in_specs = [
        pl.BlockSpec((frames, 1, part, width), lambda f: (0, f, 0, 0)),
        pl.BlockSpec((1, 1, tokens, width), lambda f: (clip, f, 0, 0)),
        full(mod.shape),
        full(w_c.shape),
        by_frame(3 * width),
        by_frame(width),
        pl.BlockSpec((None, 16, tokens), lambda f: (clip * frame_count + f, 0, 0)),
    ]
    args = [grad, x, mod, w_c, qkv, branch, totals]
    body = functools.partial(space_back_kernel, clip)
    aliases = {}
    if earlier is not None:
        in_specs += [pl.BlockSpec(memory_space=pl.ANY)] * len(earlier)
        args += list(earlier)
        aliases = {7 + number: number for number in range(len(earlier))}
        body = functools.partial(space_back_next, len(earlier), clip)
    return pl.pallas_call(
        body,
        grid=(frame_count,),
        in_specs=in_specs,
        out_specs=[
            pl.BlockSpec((1, 1, tokens, width), lambda f: (clip, f, 0, 0)),
            own(width),
            own(3 * width),
            pl.BlockSpec((8, width), lambda f: (0, 0)),
        ],
        out_shape=[
            jax.ShapeDtypeStruct(x.shape, f32),
            jax.ShapeDtypeStruct((clip_count * rows, width), bf16),
            jax.ShapeDtypeStruct((clip_count * rows, 3 * width), bf16),
            jax.ShapeDtypeStruct((8, width), f32),
        ],
        scratch_shapes=[VMEM((tokens, width), bf16)],
        input_output_aliases=aliases,
        compiler_params=pltpu.CompilerParams(vmem_limit_bytes=VMEM_LIMIT),
        cost_estimate=pl.CostEstimate(
            flops=rows * 20_000_000, bytes_accessed=rows * width * 20, transcendentals=0
        ),
    )(*args)


def shards(
    inputs, cotangent, time_steps, weight_index, ada_weight, ada_bias, space_qkv, space_out,
    space_out_bias, time_qkv, time_out, time_out_bias, up_weight, up_bias, down_weight, down_bias,
):
    clip_count, frame_count, patch_count, width = inputs.shape
    clips, frames = lax.axis_size("clip"), lax.axis_size("frame")
    owners = clips * frames
    owner = lax.axis_index("clip") * frames + lax.axis_index("frame")
    part = patch_count // frames
    rows = ada_weight.shape[0]

    embed = jax.nn.silu(embed_steps(time_steps, width)).astype(bf16)
    embed = jnp.pad(embed, ((0, 16 - clip_count), (0, 0)))
    place = lax.broadcasted_iota(jnp.int32, (width, 128), 0) - owner * rows
    lane = lax.broadcasted_iota(jnp.int32, (width, 128), 1)
    select = ((place == lane) & (lane < rows)).astype(bf16)
    ada = jnp.pad(ada_weight, ((0, 128 - rows), (0, 0)))

    def spread_bias(vector):
        length = vector.shape[0]
        empty = jnp.zeros((owners * length,), f32)
        return lax.dynamic_update_slice(empty, vector.astype(f32), (owner * length,)).reshape(
            -1, width
        )

    bias = jnp.concatenate(
        [
            spread_bias(vector)
            for vector in (ada_bias, space_out_bias, time_out_bias, up_bias, down_bias)
        ],
        axis=0,
    )
    sh_c = jnp.concatenate([space_qkv, space_out], axis=1)
    sh_b = jnp.concatenate([time_qkv, time_out], axis=1)
    (
        w_c, w_b, w_u, w_d, mod, chosen, totals, hidden_one, qkv_one, mixed_one, branch_one,
        after_first, after_later, cot_first,
    ) = start_call(
        clips, frames, inputs, cotangent, sh_c, sh_b, up_weight, down_weight, embed, select, ada,
        bias,
    )

    def exchange(values):
        return lax.all_to_all(values, "frame", split_axis=0, concat_axis=0, tiled=True)

    loss = jnp.exp2(weight_index.astype(f32) * 0.5 - 1.0)
    loss = jnp.broadcast_to(loss[:, None], (clip_count, width))
    (
        act, gup, h3, gb3, mixed_two, gb2, h2, gqkv_two, mid_sums, _, _, grad_first,
        grad_later, out_all,
    ) = middle_call(
        clips, frames, after_first, cot_first, after_later, cotangent, loss, mod, w_b, w_u, w_d
    )
    grads = [grad_first, exchange(grad_later)]

    earlier = None
    space_sums = []
    for clip in range(clip_count):
        *earlier, sums = space_back_call(
            clip, grads[clip], inputs, mod, w_c, qkv_one, branch_one, totals, earlier
        )
        space_sums.append(sums)
    input_grad, gb1, gqkv_one = earlier
    pieces = []
    for clip in range(clip_count):
        pieces += [space_sums[clip][0:3], mid_sums[clip][0:6]]
    pieces.append(sum(entry[3:4] for entry in space_sums))
    pieces.append(sum(entry[6:12] for entry in mid_sums))
    small = jnp.concatenate(pieces, axis=0)
    small = jnp.pad(small, ((0, ROWS - small.shape[0]), (0, 0)))
    picked = chosen.reshape(clips, 16, 128)[:, :clip_count].reshape(clips * clip_count, 128)
    outputs, grad_ada, sums, own_u, own_d, own_b, own_bo, own_c, own_co = grad_call(
        clips, frames, clip_count, small, picked.astype(f32).T, out_all, h3, gup, act, gb3, h2, gqkv_two,
        mixed_two, gb2, hidden_one.reshape(-1, width), gqkv_one, mixed_one.reshape(-1, width), gb1,
    )
    biases = sums[9:]

    def own_slice(vector):
        length = vector.shape[0] // owners
        return lax.dynamic_slice_in_dim(vector, owner * length, length, 0)

    return (
        outputs,
        input_grad,
        grad_ada,
        own_slice(sums[:9].reshape(-1)),
        own_c,
        own_co,
        own_slice(biases[0]),
        own_b,
        own_bo,
        own_slice(biases[1]),
        own_u,
        own_slice(biases[2:6].reshape(-1)),
        own_d,
        own_slice(biases[6]),
    )


def solution(mesh):
    tokens = P("clip", "frame", None, None)
    matrix = P(("clip", "frame"), None)
    vector = P(("clip", "frame"))
    in_specs = (
        tokens, tokens, P("clip"), P("clip"), matrix, vector, matrix, matrix, vector, matrix,
        matrix, vector, matrix, vector, matrix, vector,
    )
    out_specs = (
        tokens, tokens, matrix, vector, matrix, matrix, vector, matrix, matrix, vector, matrix,
        vector, matrix, vector,
    )
    return jax.shard_map(shards, mesh=mesh, in_specs=in_specs, out_specs=out_specs, check_vma=False)
```

profile of v0, /device:TPU:0, one launch (start us, length us, event | category | flops | bytes accessed | tf_op | source)
XLA Modules:
  0.0 503.8 jit_solution(18386923299668962206)
XLA Ops:
  0.7 0.7 convert_element_type.31
  2.1 2.3 pad.13.ada
  4.4 0.7 convert_dynamic-update-slice_fusion
  6.5 0.7 convert_dynamic-update-slice_fusion.1
  7.9 0.7 multiply_exponential_fusion.1
  8.6 1.6 pad_maximum_fusion.sh_c
  10.1 1.6 pad_maximum_fusion.1.sh_b
  11.7 0.8 fusion.1.select
  13.0 2.0 concatenate.18.bias
  15.0 127.9 %shard_map.263 = (bf16[768,3072]{1,0:T(8,128)(2,1)}, bf16[768,3072]{1,0:T(8,128)(2,1)}, bf16[768,3072]{1,0:T(8,128)(2,1)}, bf16[3072,768]{1,0:T(8,128)(2,1)}, f3...) custom-call(bf16[2,4,256,768]{3,2,1,0:T(8,128)(2,1)} %refs_1_.1, ...), custom_call_target="tpu_custom_call" | custom-call | tf_op jit(solution)/shard_map/pallas_call | solution.py:441
  143.0 0.7 broadcast_in_dim.16.loss
  143.6 142.9 %shard_map.264 = (bf16[2048,3072]{1,0:T(8,128)(2,1)}, bf16[2048,3072]{1,0:T(8,128)(2,1)}, bf16[2048,768]{1,0:T(8,128)(2,1)}, bf16[2048,768]{1,0:T(8,128)(2,1)}, ...) custom-call(bf16[4,4,64,768]{3,2,1,0:T(8,128)(2,1)} %get-tuple-eleme, ...), custom_call_target="tpu_custom_call" | custom-call | tf_op jit(solution)/shard_map/pallas_call | solution.py:1189
  286.5 5.1 %all-to-all-start = ((bf16[4,4,64,768]{3,2,1,0:T(8,128)(2,1)}), bf16[4,4,64,768]{3,2,1,0:T(8,128)(2,1)S(1)}, u32[]{:S(2)}, u32[]{:S(2)}) async-start(bf16[4,4,64,768]{3,2,1,0:T(8,128)(2,1)} %get-tuple-element.71), calls=%async_computation | async-start | bytes 3145728 | tf_op jit(solution)/shard_map/all_to_all | solution.py:1351
  291.6 31.7 %shard_map.265 = (f32[2,4,256,768]{3,2,1,0:T(8,128)}, bf16[2048,768]{1,0:T(8,128)(2,1)}, bf16[2048,2304]{1,0:T(8,128)(2,1)}, f32[8,768]{1,0:T(8,128)}) custom-call(bf16[4,4,64,768]{3,2,1,0:T(8,128)(2,1)} %get-tuple-element.64.grad_ref, bf16[2,4,256,768]{3,2,1,0:T(8,128)(2,1)} %refs_1_.1, f32[32,768]{1,0:T(8,128)} %get-tuple-element.60.mod.refs_2_, ...), custom_call_target="tpu_custom_call" | custom-call | flops 20480000000 | bytes 15728640 | tf_op jit(solution)/shard_map/pallas_call | solution.py:1283
  323.4 0.7 slice.61
  324.1 0.7 slice.77
  324.8 0.7 copy.34
  325.6 2.8 all-to-all-done.refs_0_
  328.4 1.2 copy-done
  329.5 31.7 %shard_map.266 = (f32[2,4,256,768]{3,2,1,0:T(8,128)}, bf16[2048,768]{1,0:T(8,128)(2,1)}, bf16[2048,2304]{1,0:T(8,128)(2,1)}, f32[8,768]{1,0:T(8,128)}) custom-call(bf16[4,4,64,768]{3,2,1,0:T(8,128)(2,1)} %copy-done, bf16[2,4,256,768]{3,2,1,0:T(8,128)(2,1)} %refs_1_.1, ...), custom_call_target="tpu_custom_call", output_to_operand_aliasing={{0}: (7, {}), {1}: (8, {}), {2}: (9, {})} | custom-call | flops 20480000000 | bytes 15728640 | tf_op jit(solution)/shard_map/pallas_call | solution.py:1283
  361.3 0.7 slice.64
  362.0 0.8 slice_add_fusion
  363.8 126.1 %shard_map.267 = (bf16[2,4,256,768]{3,2,1,0:T(8,128)(2,1)}, f32[24,6912]{1,0:T(8,128)}, f32[16,768]{1,0:T(8,128)}, f32[24,3072]{1,0:T(8,128)}, f32[96,768]{1,0:T...) custom-call(f32[32,768]{1,0:T(8,128)} %pad.14.small, ...), custom_call_target="tpu_custom_call" | custom-call | tf_op jit(solution)/shard_map/pallas_call | solution.py:807
  489.9 0.9 fusion.6
  490.8 0.7 slice.75
  491.5 0.8 reshape.105
  494.8 3.9 copy.52
  498.6 0.8 copy.53
  499.5 0.7 copy.54
  500.8 0.7 copy.56
  502.1 0.7 copy.58
  502.8 0.7 copy.59
  (46 shorter events, 7.9 us)
Async XLA Ops:
  286.5 41.9 %all-to-all-start = ((bf16[4,4,64,768]{3,2,1,0:T(8,128)(2,1)}), bf16[4,4,64,768]{3,2,1,0:T(8,128)(2,1)S(1)}, u32[]{:S(2)}, u32[]{:S(2)}) async-start(bf16[4,4,64,768]{3,2,1,0:T(8,128)(2,1)} %get-tuple-element.71), calls=%async_computation | async-start | bytes 3145728 | tf_op jit(solution)/shard_map/all_to_all | solution.py:1351
  291.6 33.9 %copy-start.6 = (f32[2,16,768]{2,1,0:T(8,128)S(1)}, f32[2,16,768]{2,1,0:T(8,128)}, u32[]{:S(2)}) copy-start(f32[2,16,768]{2,1,0:T(8,128)} %get-tuple-element.70) | copy-start | bytes 294916
  328.4 1.2 copy-start
  494.7 3.9 copy-start.1
  494.7 4.8 copy-start.5
  494.7 5.5 %copy-start.8 = (f32[24,768]{1,0:T(8,128)S(1)}, f32[24,768]{1,0:T(8,128)}, u32[]{:S(2)}) copy-start(f32[24,768]{1,0:T(8,128)} %get-tuple-element.129) | copy-start | bytes 221188
  494.7 6.1 %copy-start.4 = (f32[24,2304]{1,0:T(8,128)S(1)}, f32[24,2304]{1,0:T(8,128)}, u32[]{:S(2)}) copy-start(f32[24,2304]{1,0:T(8,128)} %get-tuple-element.131) | copy-start | bytes 663556
  494.7 6.8 %copy-start.7 = (f32[24,768]{1,0:T(8,128)S(1)}, f32[24,768]{1,0:T(8,128)}, u32[]{:S(2)}) copy-start(f32[24,768]{1,0:T(8,128)} %get-tuple-element.132) | copy-start | bytes 221188
  494.7 7.4 %copy-start.3 = (f32[24,3072]{1,0:T(8,128)S(1)}, f32[24,3072]{1,0:T(8,128)}, u32[]{:S(2)}) copy-start(f32[24,3072]{1,0:T(8,128)} %get-tuple-element.134) | copy-start | bytes 884740
  494.7 8.1 %copy-start.2 = (f32[96,768]{1,0:T(8,128)S(1)}, f32[96,768]{1,0:T(8,128)}, u32[]{:S(2)}) copy-start(f32[96,768]{1,0:T(8,128)} %get-tuple-element.136) | copy-start | bytes 884740
where the time goes:
time: 512 us; the launch traced here: 504 us
  Pallas kernels  460 us (90%)
  local copies, waits for them, and re-layouts  24.7 us (5%)
  other arithmetic  9.74 us (2%)
    pallas_call x1, Pallas kernels, middle_call(): pl.pallas_call(functools.partial(middle_kernel, clips, frames, tiles), gr...  143 us
    pallas_call x1, Pallas kernels, start_call(): pl.pallas_call(functools.partial(start_kernel, clips, frames, clip_count)...  128 us
    pallas_call x1, Pallas kernels, grad_call(): pl.pallas_call(functools.partial(grad_kernel, clips, frames, clip_count),...  126 us
    pallas_call x2, Pallas kernels, space_back_call(): pl.pallas_call(body, grid=(frame_count,), in_specs=in_specs, out_specs=[p...  63.4 us
  transfers between devices with their start and end apart: 1, of which 1 were waited for; matrix products, arithmetic and copies ran while one was open for 0% of the time, Pallas kernels for 6%

commit v1 on v0

--- a/solution.py
+++ b/solution.py
@@ -10,7 +10,7 @@
 
 HEADS = 12
 HEAD = 64
-PAIRS = HEADS // 2
+GROUP = 4
 ROWS = 32
 GELU_C = math.sqrt(2.0 / math.pi)
 GELU_A = 0.044715
@@ -871,61 +871,75 @@
     return jnp.sum(values, axis=0, keepdims=True)
 
 
+def head_lanes(tokens):
+    lane = lax.broadcasted_iota(jnp.int32, (tokens, GROUP * HEAD), 1)
+    return [(lane >= HEAD * head) & (lane < HEAD * (head + 1)) for head in range(GROUP)]
+
+
+def stacked(values, picks):
+    return jnp.concatenate([jnp.where(pick, values, bf16(0)) for pick in picks], axis=0)
+
+
+def unstacked(values, picks, tokens):
+    result = values[(GROUP - 1) * tokens :]
+    for head in range(GROUP - 1):
+        result = jnp.where(picks[head], values[head * tokens : (head + 1) * tokens], result)
+    return result
+
+
+def masked_scores(keys, own, mask):
+    scores = dot(keys, own, 1, 1)
+    if mask is not None:
+        scores = scores + jnp.concatenate([mask[...]] * GROUP, axis=1)
+    return scores
+
+
 def attend(qkv, mixed, totals, width, mask):
     tokens = qkv.shape[0]
-    low = lax.broadcasted_iota(jnp.int32, (tokens, 128), 1) < HEAD
-    for pair in range(PAIRS):
-        at = pair * 128
-        queries = qkv[:, at : at + 128] * bf16(0.125)
-        keys = qkv[:, width + at : width + at + 128]
-        values = qkv[:, 2 * width + at : 2 * width + at + 128]
-        halves = []
-        for half in range(2):
-            own = jnp.where(low if half == 0 else ~low, queries, bf16(0))
-            scores = dot(keys, own, 1, 1)
-            if mask is not None:
-                scores = scores + mask[...]
-            peak = jnp.max(scores, axis=0, keepdims=True)
-            terms = jnp.exp(scores - peak)
-            total = jnp.sum(terms, axis=0, keepdims=True)
-            weights = (terms * (1.0 / total)).astype(bf16)
-            totals[2 * pair + half : 2 * pair + half + 1, :] = peak + jnp.log(total)
-            halves.append(dot(weights, values, 0, 0))
-        mixed[:, at : at + 128] = jnp.where(low, halves[0], halves[1]).astype(bf16)
+    lanes = GROUP * HEAD
+    picks = head_lanes(tokens)
+    for group in range(HEADS // GROUP):
+        at = group * lanes
+        own = stacked(qkv[:, at : at + lanes] * bf16(0.125), picks)
+        keys = qkv[:, width + at : width + at + lanes]
+        values = qkv[:, 2 * width + at : 2 * width + at + lanes]
+        scores = masked_scores(keys, own, mask)
+        peak = jnp.max(scores, axis=0, keepdims=True)
+        terms = jnp.exp(scores - peak)
+        total = jnp.sum(terms, axis=0, keepdims=True)
+        weights = (terms * (1.0 / total)).astype(bf16)
+        logs = peak + jnp.log(total)
+        for head in range(GROUP):
+            row = group * GROUP + head
+            totals[row : row + 1, :] = logs[:, head * tokens : (head + 1) * tokens]
+        result = unstacked(dot(weights, values, 0, 0), picks, tokens)
+        mixed[:, at : at + lanes] = result.astype(bf16)
 
 
 def attend_back(qkv, grad_mixed, totals, grad_qkv, width, mask):
     tokens = qkv.shape[0]
-    low = lax.broadcasted_iota(jnp.int32, (tokens, 128), 1) < HEAD
-    for pair in range(PAIRS):
-        at = pair * 128
-        queries = qkv[:, at : at + 128]
-        keys = qkv[:, width + at : width + at + 128]
-        values = qkv[:, 2 * width + at : 2 * width + at + 128]
-        grads = grad_mixed[:, at : at + 128]
-        halves = []
-        for half in range(2):
-            pick = low if half == 0 else ~low
-            own = jnp.where(pick, queries * bf16(0.125), bf16(0))
-            own_grads = jnp.where(pick, grads, bf16(0))
-            scores = dot(keys, own, 1, 1)
-            if mask is not None:
-                scores = scores + mask[...]
-            weights = jnp.exp(scores - totals[2 * pair + half : 2 * pair + half + 1, :])
-            grad_weights = dot(values, own_grads, 1, 1)
-            inner = jnp.sum(weights * grad_weights, axis=0, keepdims=True)
-            grad_scores = (weights * (grad_weights - inner)).astype(bf16)
-            halves.append(
-                (
-                    dot(grad_scores, keys, 0, 0),
-                    dot(grad_scores, queries, 1, 0),
-                    dot(weights.astype(bf16), grads, 1, 0),
-                )
-            )
-        for part, factor in ((0, 0.125), (1, 0.125), (2, 1.0)):
-            joined = jnp.where(low, halves[0][part], halves[1][part]) * factor
+    lanes = GROUP * HEAD
+    picks = head_lanes(tokens)
+    for group in range(HEADS // GROUP):
+        at = group * lanes
+        own = stacked(qkv[:, at : at + lanes] * bf16(0.125), picks)
+        keys = qkv[:, width + at : width + at + lanes]
+        values = qkv[:, 2 * width + at : 2 * width + at + lanes]
+        own_grads = stacked(grad_mixed[:, at : at + lanes], picks)
+        logs = jnp.concatenate(
+            [totals[group * GROUP + head : group * GROUP + head + 1, :] for head in range(GROUP)],
+            axis=1,
+        )
+        weights = jnp.exp(masked_scores(keys, own, mask) - logs)
+        grad_weights = dot(values, own_grads, 1, 1)
+        inner = jnp.sum(weights * grad_weights, axis=0, keepdims=True)
+        grad_scores = (weights * (grad_weights - inner)).astype(bf16)
+        grad_queries = unstacked(dot(grad_scores, keys, 0, 0), picks, tokens) * 0.125
+        grad_keys = dot(grad_scores, own, 1, 0)
+        grad_values = dot(weights.astype(bf16), own_grads, 1, 0)
+        for part, grad in enumerate((grad_queries, grad_keys, grad_values)):
             start = part * width + at
-            grad_qkv[:, start : start + 128] = joined.astype(bf16)
+            grad_qkv[:, start : start + lanes] = grad.astype(bf16)
 
 
 def full(shape):

time: 512 us -> 495 us (0.967)
  Pallas kernels: 460 us -> 423 us
  starting transfers between devices: 5.1 us -> 22 us
    pallas_call x2, Pallas kernels: 63.4 us -> 44.7 us  [space_back_call(): pl.pallas_call(body, grid=(frame_count,), in_specs=in_specs, out_specs=[p...]
    all_to_all x1, starting transfers between devices: 5.1 us -> 22 us  [exchange(): lax.all_to_all(values, 'frame', split_axis=0, concat_axis=0, tiled=True)]
    pallas_call x1, Pallas kernels: 143 us -> 127 us  [middle_call(): pl.pallas_call(functools.partial(middle_kernel, clips, frames, tiles), gr...]
  transfers between devices with their start and end apart: 1 -> 1, of which waited for: 1 -> 1; matrix products, arithmetic and copies ran while one was open for 0% -> 0% of each run, Pallas kernels for 6% -> 5%
where the time goes in v1:
time: 495 us; the launch traced here: 487 us
  Pallas kernels  423 us (85%)
  local copies, waits for them, and re-layouts  24.7 us (5%)
  starting transfers between devices  22 us (4%)
  other arithmetic  9.74 us (2%)
  waiting for transfers between devices  6.28 us (1%)
    pallas_call x1, Pallas kernels, middle_call(): pl.pallas_call(functools.partial(middle_kernel, clips, frames, tiles), gr...  127 us
    pallas_call x1, Pallas kernels, start_call(): pl.pallas_call(functools.partial(start_kernel, clips, frames, clip_count)...  126 us
    pallas_call x1, Pallas kernels, grad_call(): pl.pallas_call(functools.partial(grad_kernel, clips, frames, clip_count),...  125 us
    pallas_call x2, Pallas kernels, space_back_call(): pl.pallas_call(body, grid=(frame_count,), in_specs=in_specs, out_specs=[p...  44.7 us
    all_to_all x1, starting transfers between devices, exchange(): lax.all_to_all(values, 'frame', split_axis=0, concat_axis=0, tiled=True)  22 us
    unnamed x26, local copies, waits for them, and re-layouts  9.97 us
  transfers between devices with their start and end apart: 1, of which 1 were waited for; matrix products, arithmetic and copies ran while one was open for 0% of the time, Pallas kernels for 5%

profile of v1, /device:TPU:0, one launch (start us, length us, event | category | flops | bytes accessed | tf_op | source)
XLA Modules:
  0.0 487.2 jit_solution(7458275692593656040)
XLA Ops:
  0.7 0.7 convert_element_type.31
  2.1 2.3 pad.13.ada
  4.4 0.7 convert_dynamic-update-slice_fusion
  6.5 0.7 convert_dynamic-update-slice_fusion.1
  7.9 0.7 multiply_exponential_fusion.1
  8.6 1.6 pad_maximum_fusion.sh_c
  10.1 1.6 pad_maximum_fusion.1.sh_b
  11.7 0.8 fusion.1.select
  13.0 2.0 concatenate.18.bias
  15.0 126.1 %shard_map.263 = (bf16[768,3072]{1,0:T(8,128)(2,1)}, bf16[768,3072]{1,0:T(8,128)(2,1)}, bf16[768,3072]{1,0:T(8,128)(2,1)}, bf16[3072,768]{1,0:T(8,128)(2,1)}, f3...) custom-call(bf16[2,4,256,768]{3,2,1,0:T(8,128)(2,1)} %refs_1_.1, ...), custom_call_target="tpu_custom_call" | custom-call | tf_op jit(solution)/shard_map/pallas_call | solution.py:441
  141.2 0.7 broadcast_in_dim.16.loss
  141.8 127.1 %shard_map.264 = (bf16[2048,3072]{1,0:T(8,128)(2,1)}, bf16[2048,3072]{1,0:T(8,128)(2,1)}, bf16[2048,768]{1,0:T(8,128)(2,1)}, bf16[2048,768]{1,0:T(8,128)(2,1)}, ...) custom-call(bf16[4,4,64,768]{3,2,1,0:T(8,128)(2,1)} %get-tuple-eleme, ...), custom_call_target="tpu_custom_call" | custom-call | tf_op jit(solution)/shard_map/pallas_call | solution.py:1203
  268.9 22.0 %all-to-all-start = ((bf16[4,4,64,768]{3,2,1,0:T(8,128)(2,1)}), bf16[4,4,64,768]{3,2,1,0:T(8,128)(2,1)S(1)}, u32[]{:S(2)}, u32[]{:S(2)}) async-start(bf16[4,4,64,768]{3,2,1,0:T(8,128)(2,1)} %get-tuple-element.71), calls=%async_computation | async-start | bytes 3145728 | tf_op jit(solution)/shard_map/all_to_all | solution.py:1365
  291.0 22.3 %shard_map.265 = (f32[2,4,256,768]{3,2,1,0:T(8,128)}, bf16[2048,768]{1,0:T(8,128)(2,1)}, bf16[2048,2304]{1,0:T(8,128)(2,1)}, f32[8,768]{1,0:T(8,128)}) custom-call(bf16[4,4,64,768]{3,2,1,0:T(8,128)(2,1)} %get-tuple-element.64.grad_ref, bf16[2,4,256,768]{3,2,1,0:T(8,128)(2,1)} %refs_1_.1, f32[32,768]{1,0:T(8,128)} %get-tuple-element.60.mod.refs_2_, ...), custom_call_target="tpu_custom_call" | custom-call | flops 20480000000 | bytes 15728640 | tf_op jit(solution)/shard_map/pallas_call | solution.py:1297
  313.3 0.7 slice.61
  314.1 0.7 slice.77
  314.8 0.7 copy.34
  315.5 6.3 %all-to-all-done.refs_0_ = bf16[4,4,64,768]{3,2,1,0:T(8,128)(2,1)S(1)} async-done(((bf16[4,4,64,768]{3,2,1,0:T(8,128)(2,1)}), bf16[4,4,64,768]{3,2,1,0:T(8,128)(2,1)S(1)}, u32[]{:S(2)}, u32[]{:S(2)}) %all-to-all-start) | async-done | bytes 1572896 | tf_op jit(solution)/shard_map/all_to_all | solution.py:1365
  321.8 1.2 copy-done
  323.0 22.3 %shard_map.266 = (f32[2,4,256,768]{3,2,1,0:T(8,128)}, bf16[2048,768]{1,0:T(8,128)(2,1)}, bf16[2048,2304]{1,0:T(8,128)(2,1)}, f32[8,768]{1,0:T(8,128)}) custom-call(bf16[4,4,64,768]{3,2,1,0:T(8,128)(2,1)} %copy-done, bf16[2,4,256,768]{3,2,1,0:T(8,128)(2,1)} %refs_1_.1, ...), custom_call_target="tpu_custom_call", output_to_operand_aliasing={{0}: (7, {}), {1}: (8, {}), {2}: (9, {})} | custom-call | flops 20480000000 | bytes 15728640 | tf_op jit(solution)/shard_map/pallas_call | solution.py:1297
  345.3 0.7 slice.64
  346.0 0.8 slice_add_fusion
  347.8 125.5 %shard_map.267 = (bf16[2,4,256,768]{3,2,1,0:T(8,128)(2,1)}, f32[24,6912]{1,0:T(8,128)}, f32[16,768]{1,0:T(8,128)}, f32[24,3072]{1,0:T(8,128)}, f32[96,768]{1,0:T...) custom-call(f32[32,768]{1,0:T(8,128)} %pad.14.small, ...), custom_call_target="tpu_custom_call" | custom-call | tf_op jit(solution)/shard_map/pallas_call | solution.py:807
  473.3 0.9 fusion.6
  474.1 0.7 slice.75
  474.9 0.8 reshape.105
  478.1 3.9 copy.52
  482.0 0.8 copy.53
  482.9 0.7 copy.54
  484.2 0.7 copy.56
  485.5 0.7 copy.58
  486.2 0.7 copy.59
  (46 shorter events, 7.9 us)
Async XLA Ops:
  268.9 52.9 %all-to-all-start = ((bf16[4,4,64,768]{3,2,1,0:T(8,128)(2,1)}), bf16[4,4,64,768]{3,2,1,0:T(8,128)(2,1)S(1)}, u32[]{:S(2)}, u32[]{:S(2)}) async-start(bf16[4,4,64,768]{3,2,1,0:T(8,128)(2,1)} %get-tuple-element.71), calls=%async_computation | async-start | bytes 3145728 | tf_op jit(solution)/shard_map/all_to_all | solution.py:1365
  291.0 24.5 %copy-start.6 = (f32[2,16,768]{2,1,0:T(8,128)S(1)}, f32[2,16,768]{2,1,0:T(8,128)}, u32[]{:S(2)}) copy-start(f32[2,16,768]{2,1,0:T(8,128)} %get-tuple-element.70) | copy-start | bytes 294916
  321.8 1.2 copy-start
  478.1 3.9 copy-start.1
  478.1 4.8 copy-start.5
  478.1 5.5 %copy-start.8 = (f32[24,768]{1,0:T(8,128)S(1)}, f32[24,768]{1,0:T(8,128)}, u32[]{:S(2)}) copy-start(f32[24,768]{1,0:T(8,128)} %get-tuple-element.129) | copy-start | bytes 221188
  478.1 6.1 %copy-start.4 = (f32[24,2304]{1,0:T(8,128)S(1)}, f32[24,2304]{1,0:T(8,128)}, u32[]{:S(2)}) copy-start(f32[24,2304]{1,0:T(8,128)} %get-tuple-element.131) | copy-start | bytes 663556
  478.1 6.8 %copy-start.7 = (f32[24,768]{1,0:T(8,128)S(1)}, f32[24,768]{1,0:T(8,128)}, u32[]{:S(2)}) copy-start(f32[24,768]{1,0:T(8,128)} %get-tuple-element.132) | copy-start | bytes 221188
  478.1 7.4 %copy-start.3 = (f32[24,3072]{1,0:T(8,128)S(1)}, f32[24,3072]{1,0:T(8,128)}, u32[]{:S(2)}) copy-start(f32[24,3072]{1,0:T(8,128)} %get-tuple-element.134) | copy-start | bytes 884740
  478.1 8.1 %copy-start.2 = (f32[96,768]{1,0:T(8,128)S(1)}, f32[96,768]{1,0:T(8,128)}, u32[]{:S(2)}) copy-start(f32[96,768]{1,0:T(8,128)} %get-tuple-element.136) | copy-start | bytes 884740

commit v2 on v1

--- a/solution.py
+++ b/solution.py
@@ -283,8 +283,8 @@
         frame_rest(group)
 
     cot_copies = []
-    for step in range(1, frames):
-        peer = lax.rem(frame + step, frames)
+    for step in range(frames - 1, 0, -1):
+        peer = flip(frame, step)
         copy = pltpu.make_async_remote_copy(
             src_ref=cotangent.at[0, :, pl.ds(pl.multiple_of(peer * part, part), part), :],
             dst_ref=cot_first.at[frame],
@@ -321,7 +321,7 @@
     local_copies.append(keep)
 
     def after_copy(f, step):
-        peer = lax.rem(frame + step, frames)
+        peer = flip(frame, step)
         return pltpu.make_async_remote_copy(
             src_ref=after.at[f, pl.ds(pl.multiple_of(peer * part, part), part), :],
             dst_ref=after_first.at[frame, f],
@@ -365,7 +365,7 @@
             branch[f] = grown.astype(bf16)
             after[f] = (values + mod[row + 2 : row + 3, :] * grown).astype(bf16)
             if local == 0:
-                for step in range(1, frames):
+                for step in range(frames - 1, 0, -1):
                     after_copy(f, step).start()
                 own_after(f).start()
             else:
@@ -516,8 +516,8 @@
 
     def send_output(number):
         local, index = divmod(number, frame_count)
-        for hop in range(1, frames):
-            peer = lax.rem(frame + hop, frames)
+        for hop in range(frames - 1, 0, -1):
+            peer = flip(frame, hop)
             copy = pltpu.make_async_remote_copy(
                 src_ref=out_all.at[local, peer, index],
                 dst_ref=outputs.at[local, index, mine, :],
@@ -950,9 +950,9 @@
     clips, frames, tiles,
     after_first, cot_first, after_later, cotangent, loss, mod, w_b, w_u, w_d,
     act_ref, gup_ref, h3_ref, gb3_ref, mixed_ref, gb2_ref, h2_ref, gqkv_ref, sums,
-    after_second, cot_second, grad_first, grad_later, out_all,
+    after_second, cot_second, grad_first, grad_second, grad_later, out_all,
     qkv, totals, mask, gmix, after_tile, cot_tile, grad_stage, out_stage,
-    ts, tr, us, ur, gs, gr, ls, ks, ws,
+    ts, tr, us, ur, gs, gr, hs, hr, ls, ks, ws,
 ):
     frame = lax.axis_index("frame")
     step = pl.program_id(0)
@@ -972,8 +972,8 @@
 
     def later_copies(number):
         copies = []
-        for hop in range(1, frames):
-            peer = lax.rem(frame + hop, frames)
+        for hop in range(frames - 1, 0, -1):
+            peer = flip(frame, hop)
             if number:
                 source, target, send, recv = cotangent.at[1, :, own_part(peer), :], cot_second, us, ur
             else:
@@ -1002,32 +1002,38 @@
         target = (after_tile, cot_tile)[number].at[place]
         return pltpu.make_async_copy(source.at[:, :, rows, :], target, ls.at[place, number])
 
-    def grad_copies(index):
+    early = tiles // 2
+
+    def grad_copies(index, later=False):
+        place = index + tiles if later else index
+        target, send, recv = (grad_second, hs, hr) if later else (grad_first, gs, gr)
         rows = pl.ds(pl.multiple_of(index * group, group), group)
         copies = []
-        for hop in range(1, frames):
-            peer = lax.rem(frame + hop, frames)
+        for hop in range(frames - 1, 0, -1):
+            peer = flip(frame, hop)
             copies.append(
                 pltpu.make_async_remote_copy(
-                    src_ref=grad_stage.at[index, peer],
-                    dst_ref=grad_first.at[frame, :, rows, :],
-                    send_sem=gs.at[index, hop - 1],
-                    recv_sem=gr.at[index, hop - 1],
+                    src_ref=grad_stage.at[place, peer],
+                    dst_ref=target.at[frame, :, rows, :],
+                    send_sem=send.at[index, hop - 1],
+                    recv_sem=recv.at[index, hop - 1],
                     device_id={"frame": peer},
                     device_id_type=MESH,
                 )
             )
         return copies
 
-    def grad_own(index):
+    def grad_own(index, later=False):
+        place = index + tiles if later else index
+        target = grad_second if later else grad_first
         rows = pl.ds(pl.multiple_of(index * group, group), group)
         return pltpu.make_async_copy(
-            grad_stage.at[index, frame], grad_first.at[frame, :, rows, :], ws.at[0, index]
+            grad_stage.at[place, frame], target.at[frame, :, rows, :], ws.at[0, place]
         )
 
     def grad_keep(index):
         place = index + tiles
-        rows = pl.ds(pl.multiple_of(index * group, group), group)
+        rows = pl.ds(pl.multiple_of((index - early) * group, group), group)
         return pltpu.make_async_copy(
             grad_stage.at[place], grad_later.at[:, :, rows, :], ws.at[0, place]
         )
@@ -1164,7 +1170,15 @@
     def _():
         grad_own(tile).start()
 
-    @pl.when(step >= tiles)
+    if early:
+
+        @pl.when((step >= tiles) & (tile < early))
+        def _():
+            for copy in grad_copies(tile, True):
+                copy.start()
+            grad_own(tile, True).start()
+
+    @pl.when((step >= tiles) & (tile >= early))
     def _():
         grad_keep(tile).start()
 
@@ -1178,12 +1192,27 @@
                 copy.wait_send()
                 copy.wait_recv()
             grad_own(index).wait()
-            grad_keep(index).wait()
             out_keep(index).wait()
             out_keep(index + tiles).wait()
             return carry
 
         lax.fori_loop(0, tiles, settle, 0)
+
+        def settle_early(index, carry):
+            for copy in grad_copies(index, True):
+                copy.wait_send()
+                copy.wait_recv()
+            grad_own(index, True).wait()
+            return carry
+
+        if early:
+            lax.fori_loop(0, early, settle_early, 0)
+
+        def settle_kept(index, carry):
+            grad_keep(index).wait()
+            return carry
+
+        lax.fori_loop(early, tiles, settle_kept, 0)
 
 
 def middle_call(
@@ -1209,11 +1238,14 @@
         ],
         out_specs=[own(columns) for columns in widths]
         + [pl.BlockSpec((None, 16, width), lambda t: (t // tiles, 0, 0))]
-        + [hbm] * 5,
+        + [hbm] * 6,
         out_shape=[jax.ShapeDtypeStruct((rows, columns), bf16) for columns in widths]
         + [
             jax.ShapeDtypeStruct((2, 16, width), f32),
             traded, traded, traded, traded,
+            jax.ShapeDtypeStruct(
+                (frames, frame_count, part - tiles // 2 * group, width), bf16
+            ),
             jax.ShapeDtypeStruct((2,) + after_first.shape, bf16),
         ],
         scratch_shapes=[
@@ -1228,6 +1260,7 @@
             DMA((frames - 1,)), DMA((frames - 1,)),
             DMA((frames - 1,)), DMA((frames - 1,)),
             DMA((tiles, frames - 1)), DMA((tiles, frames - 1)),
+            DMA((max(tiles // 2, 1), frames - 1)), DMA((max(tiles // 2, 1), frames - 1)),
             DMA((2, 2)), DMA((2,)), DMA((2, 2 * tiles)),
         ],
         compiler_params=pltpu.CompilerParams(
@@ -1237,7 +1270,7 @@
 
 
 def space_back_kernel(
-    clip, grad_ref, x_ref, mod, w_c, qkv, branch, totals,
+    clip, grad_refs, x_ref, mod, w_c, qkv, branch, totals,
     out_ref, gb_ref, gqkv_ref, sums, gmix,
 ):
     width = x_ref.shape[-1]
@@ -1249,7 +1282,9 @@
     def _():
         sums[...] = jnp.zeros_like(sums)
 
-    grad = grad_ref[...].reshape(tokens, width).astype(f32)
+    joined = [grad_ref[...] for grad_ref in grad_refs]
+    joined = joined[0] if len(joined) == 1 else jnp.concatenate(joined, axis=2)
+    grad = joined.reshape(tokens, width).astype(f32)
     grad_branch = (grad * piece(2)).astype(bf16)
     gb_ref[...] = grad_branch
     sums[2:3, :] += column_sum(grad * branch[...].astype(f32))
@@ -1264,21 +1299,27 @@
     out_ref[...] = result.reshape(out_ref.shape)
 
 
-def space_back_next(count, clip, *refs):
-    space_back_kernel(clip, *refs[:7], *refs[7 + count :])
+def space_back_entry(count, parts, clip, *refs):
+    base = 6 + parts
+    space_back_kernel(clip, refs[:parts], *refs[parts:base], *refs[base + count :])
 
 
 def space_back_call(clip, grad, x, mod, w_c, qkv, branch, totals, earlier):
     clip_count, frame_count, tokens, width = x.shape
-    frames = grad.shape[0]
-    part = grad.shape[2]
+    frames = grad[0].shape[0]
+    part = tokens // frames
+    rest = [entry.shape[2] for entry in grad[1:]]
+    heights = [part - sum(rest)] + rest
+    if heights[0] == 0:
+        grad, heights = grad[1:], heights[1:]
     rows = frame_count * tokens
     by_frame = lambda columns: pl.BlockSpec(
         (None, tokens, columns), lambda f: (clip * frame_count + f, 0, 0)
     )
     own = lambda columns: pl.BlockSpec((tokens, columns), lambda f: (clip * frame_count + f, 0))
     in_specs = [
-        pl.BlockSpec((frames, 1, part, width), lambda f: (0, f, 0, 0)),
+        pl.BlockSpec((frames, 1, height, width), lambda f: (0, f, 0, 0)) for height in heights
+    ] + [
         pl.BlockSpec((1, 1, tokens, width), lambda f: (clip, f, 0, 0)),
         full(mod.shape),
         full(w_c.shape),
@@ -1286,14 +1327,14 @@
         by_frame(width),
         pl.BlockSpec((None, 16, tokens), lambda f: (clip * frame_count + f, 0, 0)),
     ]
-    args = [grad, x, mod, w_c, qkv, branch, totals]
-    body = functools.partial(space_back_kernel, clip)
+    args = list(grad) + [x, mod, w_c, qkv, branch, totals]
+    begin = len(args)
+    body = functools.partial(space_back_entry, len(earlier or ()), len(grad), clip)
     aliases = {}
     if earlier is not None:
         in_specs += [pl.BlockSpec(memory_space=pl.ANY)] * len(earlier)
         args += list(earlier)
-        aliases = {7 + number: number for number in range(len(earlier))}
-        body = functools.partial(space_back_next, len(earlier), clip)
+        aliases = {begin + number: number for number in range(len(earlier))}
     return pl.pallas_call(
         body,
         grid=(frame_count,),
@@ -1368,11 +1409,11 @@
     loss = jnp.broadcast_to(loss[:, None], (clip_count, width))
     (
         act, gup, h3, gb3, mixed_two, gb2, h2, gqkv_two, mid_sums, _, _, grad_first,
-        grad_later, out_all,
+        grad_second, grad_later, out_all,
     ) = middle_call(
         clips, frames, after_first, cot_first, after_later, cotangent, loss, mod, w_b, w_u, w_d
     )
-    grads = [grad_first, exchange(grad_later)]
+    grads = [(grad_first,), (grad_second, exchange(grad_later))]
 
     earlier = None
     space_sums = []

time: 495 us -> 475 us (0.960)
  starting transfers between devices: 22 us -> 3.67 us
  waiting for transfers between devices: 6.28 us -> 0.01 us
  Pallas kernels: 423 us -> 428 us
    all_to_all x1, starting transfers between devices: 22 us -> 3.67 us  [exchange(): lax.all_to_all(values, 'frame', split_axis=0, concat_axis=0, tiled=True)]
    pallas_call x1, Pallas kernels: 127 us -> 136 us  [middle_call(): pl.pallas_call(functools.partial(middle_kernel, clips, frames, tiles), gr...]
    all_to_all x1, waiting for transfers between devices: 6.28 us -> 0.01 us  [exchange(): lax.all_to_all(values, 'frame', split_axis=0, concat_axis=0, tiled=True)]
    pallas_call x1, Pallas kernels: 126 us -> 120 us  [start_call(): pl.pallas_call(functools.partial(start_kernel, clips, frames, clip_count)...]
  transfers between devices with their start and end apart: 1 -> 1, of which waited for: 1 -> 0; matrix products, arithmetic and copies ran while one was open for 0% -> 0% of each run, Pallas kernels for 5% -> 5%
where the time goes in v2:
time: 475 us; the launch traced here: 467 us
  Pallas kernels  428 us (90%)
  local copies, waits for them, and re-layouts  24.5 us (5%)
  other arithmetic  9.74 us (2%)
    pallas_call x1, Pallas kernels, middle_call(): pl.pallas_call(functools.partial(middle_kernel, clips, frames, tiles), gr...  136 us
    pallas_call x1, Pallas kernels, grad_call(): pl.pallas_call(functools.partial(grad_kernel, clips, frames, clip_count),...  127 us
    pallas_call x1, Pallas kernels, start_call(): pl.pallas_call(functools.partial(start_kernel, clips, frames, clip_count)...  120 us
    pallas_call x2, Pallas kernels, space_back_call(): pl.pallas_call(body, grid=(frame_count,), in_specs=in_specs, out_specs=[p...  44.7 us
    unnamed x26, local copies, waits for them, and re-layouts  9.72 us
  transfers between devices with their start and end apart: 1, of which 0 were waited for; matrix products, arithmetic and copies ran while one was open for 0% of the time, Pallas kernels for 5%

profile of v2, /device:TPU:0, one launch (start us, length us, event | category | flops | bytes accessed | tf_op | source)
XLA Modules:
  0.0 466.6 jit_solution(8458821742127039618)
XLA Ops:
  0.7 0.7 convert_element_type.31
  2.1 2.3 pad.13.ada
  4.4 0.7 convert_dynamic-update-slice_fusion
  5.2 0.7 bitcast_convert_fusion.2
  6.5 0.7 convert_dynamic-update-slice_fusion.1
  7.9 0.7 multiply_exponential_fusion.1
  8.6 1.6 pad_maximum_fusion.sh_c
  10.1 1.6 pad_maximum_fusion.1.sh_b
  11.7 0.8 fusion.1.select
  13.0 2.0 concatenate.18.bias
  15.0 119.9 %shard_map.263 = (bf16[768,3072]{1,0:T(8,128)(2,1)}, bf16[768,3072]{1,0:T(8,128)(2,1)}, bf16[768,3072]{1,0:T(8,128)(2,1)}, bf16[3072,768]{1,0:T(8,128)(2,1)}, f3...) custom-call(bf16[2,4,256,768]{3,2,1,0:T(8,128)(2,1)} %refs_2_.1, ...), custom_call_target="tpu_custom_call" | custom-call | tf_op jit(solution)/shard_map/pallas_call | solution.py:441
  134.9 0.7 broadcast_in_dim.16.loss
  135.6 135.8 %shard_map.264 = (bf16[2048,3072]{1,0:T(8,128)(2,1)}, bf16[2048,3072]{1,0:T(8,128)(2,1)}, bf16[2048,768]{1,0:T(8,128)(2,1)}, bf16[2048,768]{1,0:T(8,128)(2,1)}, ...) custom-call(bf16[4,4,64,768]{3,2,1,0:T(8,128)(2,1)} %get-tuple-eleme, ...), custom_call_target="tpu_custom_call" | custom-call | tf_op jit(solution)/shard_map/pallas_call | solution.py:1232
  271.4 3.7 all-to-all-start
  275.1 22.3 %shard_map.265 = (f32[2,4,256,768]{3,2,1,0:T(8,128)}, bf16[2048,768]{1,0:T(8,128)(2,1)}, bf16[2048,2304]{1,0:T(8,128)(2,1)}, f32[8,768]{1,0:T(8,128)}) custom-call(bf16[4,4,64,768]{3,2,1,0:T(8,128)(2,1)} %get-tuple-element.65.refs_0_, bf16[2,4,256,768]{3,2,1,0:T(8,128)(2,1)} %refs_2_.1, f32[32,768]{1,0:T(8,128)} %get-tuple-element.61.mod.refs_2_.refs_3_, ...), custom_call_target="tpu_custom_call" | custom-call | flops 20480000000 | bytes 15728640 | tf_op jit(solution)/shard_map/pallas_call | solution.py:1338
  297.4 0.7 slice.61
  298.2 0.7 slice.77
  298.9 0.7 copy.34
  299.7 0.9 copy-done
  300.6 22.3 %shard_map.266 = (f32[2,4,256,768]{3,2,1,0:T(8,128)}, bf16[2048,768]{1,0:T(8,128)(2,1)}, bf16[2048,2304]{1,0:T(8,128)(2,1)}, f32[8,768]{1,0:T(8,128)}) custom-call(bf16[4,4,64,768]{3,2,1,0:T(8,128)(2,1)} %get-tuple-element.72.refs_0_, bf16[4,4,32,768]{3,2,1,0:T(8,128)(2,1)} %copy-done, ...), custom_call_target="tpu_custom_call", output_to_operand_aliasing={{0}: (8, {}), {1}: (9, {}), {2}: (10, {})} | custom-call | flops 20480000000 | bytes 15728640 | tf_op jit(solution)/shard_map/pallas_call | solution.py:1338
  322.9 0.7 slice.64
  323.6 0.8 slice_add_fusion
  325.4 127.3 %shard_map.267 = (bf16[2,4,256,768]{3,2,1,0:T(8,128)(2,1)}, f32[24,6912]{1,0:T(8,128)}, f32[16,768]{1,0:T(8,128)}, f32[24,3072]{1,0:T(8,128)}, f32[96,768]{1,0:T...) custom-call(f32[32,768]{1,0:T(8,128)} %pad.14.small, ...), custom_call_target="tpu_custom_call" | custom-call | tf_op jit(solution)/shard_map/pallas_call | solution.py:807
  452.7 0.9 fusion.6
  453.6 0.7 slice.75
  454.3 0.8 reshape.105
  457.6 3.9 copy.52
  461.4 0.8 copy.53
  462.3 0.7 copy.54
  463.6 0.7 copy.56
  464.9 0.7 copy.58
  465.6 0.7 copy.59
  (46 shorter events, 7.2 us)
Async XLA Ops:
  271.4 28.2 %all-to-all-start = ((bf16[4,4,32,768]{3,2,1,0:T(8,128)(2,1)}), bf16[4,4,32,768]{3,2,1,0:T(8,128)(2,1)S(1)}, u32[]{:S(2)}, u32[]{:S(2)}) async-start(bf16[4,4,32,768]{3,2,1,0:T(8,128)(2,1)} %get-tuple-element.73), calls=%async_computation | async-start | bytes 1572864 | tf_op jit(solution)/shard_map/all_to_all | solution.py:1406
  275.1 24.5 %copy-start.6 = (f32[2,16,768]{2,1,0:T(8,128)S(1)}, f32[2,16,768]{2,1,0:T(8,128)}, u32[]{:S(2)}) copy-start(f32[2,16,768]{2,1,0:T(8,128)} %get-tuple-element.71) | copy-start | bytes 294916
  299.7 0.9 copy-start
  457.5 3.9 copy-start.1
  457.5 4.8 %copy-start.5 = (f32[24,2304]{1,0:T(8,128)S(1)}, f32[24,2304]{1,0:T(8,128)}, u32[]{:S(2)}) copy-start(f32[24,2304]{1,0:T(8,128)} %get-tuple-element.130) | copy-start | bytes 663556
  457.5 5.5 %copy-start.8 = (f32[24,768]{1,0:T(8,128)S(1)}, f32[24,768]{1,0:T(8,128)}, u32[]{:S(2)}) copy-start(f32[24,768]{1,0:T(8,128)} %get-tuple-element.131) | copy-start | bytes 221188
  457.5 6.1 %copy-start.4 = (f32[24,2304]{1,0:T(8,128)S(1)}, f32[24,2304]{1,0:T(8,128)}, u32[]{:S(2)}) copy-start(f32[24,2304]{1,0:T(8,128)} %get-tuple-element.133) | copy-start | bytes 663556
  457.5 6.8 %copy-start.7 = (f32[24,768]{1,0:T(8,128)S(1)}, f32[24,768]{1,0:T(8,128)}, u32[]{:S(2)}) copy-start(f32[24,768]{1,0:T(8,128)} %get-tuple-element.134) | copy-start | bytes 221188
  457.5 7.4 %copy-start.3 = (f32[24,3072]{1,0:T(8,128)S(1)}, f32[24,3072]{1,0:T(8,128)}, u32[]{:S(2)}) copy-start(f32[24,3072]{1,0:T(8,128)} %get-tuple-element.136) | copy-start | bytes 884740
  457.5 8.1 %copy-start.2 = (f32[96,768]{1,0:T(8,128)S(1)}, f32[96,768]{1,0:T(8,128)}, u32[]{:S(2)}) copy-start(f32[96,768]{1,0:T(8,128)} %get-tuple-element.138) | copy-start | bytes 884740

commit v3 on v2

--- a/solution.py
+++ b/solution.py
@@ -107,15 +107,14 @@
 
 def start_kernel(
     clips, frames, clip_count,
-    x_ref, cotangent, sh_c, sh_b, sh_u, sh_d, embed, select, ada, bias,
+    x_ref, cotangent, sq, so, tq, to, sh_u, sh_d, embed, select, ada, bias,
     w_c, w_b, w_u, w_d, mod, chosen, totals, hidden_out, qkv_out, mixed_out, branch_out,
     after_first, after_later, cot_first,
     v_c, z_c, z_b, z_u, z_d, st_w, b_c, b_b, b_u, b_d,
-    embeds, parts, terms, arrived, held, lined, hidden, qkv, mixed, branch, after,
+    ada_full, embeds, parts, terms, arrived, held, lined, hidden, qkv, mixed, branch, after,
     zs, zr, cs, cr, xs, xr, ls, es, er, ps, pr, fs, fr, ts, tr, hs, hr, os, ws,
 ):
     clip, frame = lax.axis_index("clip"), lax.axis_index("frame")
-    shards_in = (sh_c, sh_b, sh_u, sh_d)
     zoned = (z_c, z_b, z_u, z_d)
     blocks = (b_c, b_b, b_u, b_d)
     wholes = (v_c, w_b, w_u, w_d)
@@ -132,9 +131,8 @@
         copies = []
         for offset in span(masks[:step]):
             slot = flip(frame, offset)
-            source = shards_in[group] if offset == 0 else zoned[group].at[slot]
             copy = pltpu.make_async_remote_copy(
-                src_ref=source,
+                src_ref=zoned[group].at[slot],
                 dst_ref=zoned[group].at[slot],
                 send_sem=zs.at[group, number],
                 recv_sem=zr.at[group, number],
@@ -200,7 +198,7 @@
     def block_ready(group):
         for copy in stage[group]:
             copy.wait_recv()
-        rows, columns = shards_in[group].shape
+        rows, columns = zoned[group].shape[1:]
         block_rows = frames * rows
         if rows % 16:
             for slot in range(frames):
@@ -240,18 +238,42 @@
         for copy in core_copies[group]:
             copy.wait_recv()
 
+    for group, first, second in ((0, sq, so), (1, tq, to)):
+        zoned[group][frame, :, : 3 * width] = first[...]
+        zoned[group][frame, :, 3 * width :] = second[...]
     frame_step(0, 0)
     own = spread("clip", clips, lambda peer: embed, embeds, es, er)
     sends.extend(own)
     embeds[clip] = embed[...]
-    for group in range(4):
-        zoned[group][frame] = shards_in[group][...]
+    z_u[frame] = sh_u[...]
+    z_d[frame] = sh_d[...]
+    ada_full[...] = jnp.zeros_like(ada_full)
+    ada_full[: ada.shape[0], :] = ada[...]
     frame_rest(0)
+    for group in range(1, 4):
+        frame_step(group, 0)
+    cot_copies = []
+
+    def cot_send(index):
+        for step in range(frames - 1, 0, -1):
+            peer = flip(frame, step)
+            copy = pltpu.make_async_remote_copy(
+                src_ref=cotangent.at[0, index, pl.ds(pl.multiple_of(peer * part, part), part), :],
+                dst_ref=cot_first.at[frame, index],
+                send_sem=ts.at[index, step - 1],
+                recv_sem=tr.at[index, step - 1],
+                device_id={"frame": peer},
+                device_id_type=MESH,
+            )
+            copy.start()
+            cot_copies.append(copy)
+
+    cot_send(0)
     for copy in own:
         copy.wait_recv()
     picked = dot(embeds[...].reshape(clips * 16, width), select[...], 1, 0).astype(bf16)
     chosen[...] = picked
-    parts[...] = dot(picked, ada[...], 1, 0)
+    parts[...] = dot(picked, ada_full[...], 1, 0)
     for peer in range(clips):
         for local in range(clip_count):
             row = peer * 16 + local
@@ -268,8 +290,6 @@
     sends.extend(own)
     arrived[clip] = terms[clip]
     block_ready(0)
-    for group in range(1, 4):
-        frame_step(group, 0)
     for copy in own:
         copy.wait_recv()
     total = arrived[0]
@@ -282,19 +302,8 @@
     for group in range(1, 4):
         frame_rest(group)
 
-    cot_copies = []
-    for step in range(frames - 1, 0, -1):
-        peer = flip(frame, step)
-        copy = pltpu.make_async_remote_copy(
-            src_ref=cotangent.at[0, :, pl.ds(pl.multiple_of(peer * part, part), part), :],
-            dst_ref=cot_first.at[frame],
-            send_sem=ts.at[step - 1],
-            recv_sem=tr.at[step - 1],
-            device_id={"frame": peer},
-            device_id_type=MESH,
-        )
-        copy.start()
-        cot_copies.append(copy)
+    for index in range(1, frame_count):
+        cot_send(index)
     keep = pltpu.make_async_copy(
         cotangent.at[0, :, pl.ds(pl.multiple_of(frame * part, part), part), :],
         cot_first.at[frame],
@@ -421,10 +430,10 @@
 
 
 def start_call(
-    clips, frames, inputs, cotangent, sh_c, sh_b, sh_u, sh_d, embed, select, ada, bias
+    clips, frames, inputs, cotangent, sq, so, tq, to, sh_u, sh_d, embed, select, ada, bias
 ):
     clip_count, frame_count, tokens, width = inputs.shape
-    rows, columns = sh_c.shape
+    rows, columns = sh_u.shape
     rows_d = sh_d.shape[0]
     block = frames * rows
     block_d = frames * rows_d
@@ -451,7 +460,7 @@
             jax.ShapeDtypeStruct(((clip_count - 1) * frame_count, tokens, width), bf16),
             traded,
         ),
-        in_specs=[vmem, hbm] + [vmem] * 8,
+        in_specs=[vmem, hbm] + [vmem] * 10,
         out_specs=(hbm, hbm, hbm, hbm, vmem, vmem, vmem) + (hbm,) * 7,
         scratch_shapes=[
             VMEM((clips * block, columns), bf16),
@@ -461,6 +470,7 @@
             VMEM((block, columns), bf16),
             VMEM((block, columns), bf16),
             VMEM((block_d, width), bf16),
+            VMEM((128, 9 * width), bf16),
             VMEM((clips, 16, width), bf16),
             VMEM((clips * 16, 9 * width), f32),
             VMEM((clips, ROWS, width), f32),
@@ -475,7 +485,7 @@
             DMA((clips - 1,)), DMA((clips - 1,)),
             DMA((clips - 1,)), DMA((clips - 1,)),
             DMA((frames - 1,)), DMA((frames - 1,)),
-            DMA((frames - 1,)), DMA((frames - 1,)),
+            DMA((frame_count, frames - 1)), DMA((frame_count, frames - 1)),
             DMA((frame_count, frames - 1)), DMA((frame_count, frames - 1)),
             DMA((total,)),
             DMA((4, total)),
@@ -483,7 +493,7 @@
         compiler_params=pltpu.CompilerParams(
             collective_id=0, has_side_effects=True, vmem_limit_bytes=VMEM_LIMIT
         ),
-    )(inputs, cotangent, sh_c, sh_b, sh_u, sh_d, embed, select, ada, bias)
+    )(inputs, cotangent, sq, so, tq, to, sh_u, sh_d, embed, select, ada, bias)
 
 
 STEP = 512
@@ -494,7 +504,8 @@
     clips, frames, clip_count,
     small, chosen, out_all, h3, gup, act, gb3, h2, gqkv2, mix2, gb2, h1, gqkv1, mix1, gb1,
     outputs, grad_ada, bias_sums, out_u, out_d, out_b, out_bo, out_c, out_co,
-    sum_w, sum_d, core_w, core_d, side_w, side_d, line_w, line_d, last_w, last_d,
+    sum_w, sum_d, sum_s, core_w, core_d, core_s, side_w, side_d, side_s,
+    line_w, line_d, line_s, last_w, last_d, last_s,
     left, right, total, gathered, lined, held,
     lsem, rsem, cs, cr, xs, xr, zs, zr, fs, fr, ps, pr, os, orr, ks,
 ):
@@ -545,10 +556,12 @@
         (0, 2, [(h2, gqkv2, 0, 0, wide)], out_b, 0),
         (0, 3, [(h2, gqkv2, wide, 0, width), (mix2, gb2, 0, width, width)], out_b, wide),
         (0, 4, [(h1, gqkv1, 0, 0, wide)], out_c, 0),
-        (0, 5, [(h1, gqkv1, wide, 0, width), (mix1, gb1, 0, width, width)], out_c, wide),
+        (2, 0, [(h1, gqkv1, wide, 0, width)], out_c, wide),
+        (2, 1, [(mix1, gb1, 0, 0, width)], out_co, 0),
     ]
-    sums, cores, sides = (sum_w, sum_d), (core_w, core_d), (side_w, side_d)
-    lines, lasts = (line_w, line_d), (last_w, last_d)
+    sums, cores = (sum_w, sum_d, sum_s), (core_w, core_d, core_s)
+    sides = (side_w, side_d, side_s)
+    lines, lasts = (line_w, line_d, line_s), (last_w, last_d, last_s)
     flights = {}
 
     steps = tokens // STEP
@@ -633,7 +646,7 @@
         flights[number, "core"] = copies
 
     def half_of(kind, half):
-        if kind:
+        if kind == 1:
             rows = sums[kind].shape[2] // 2
             return (slice(half * rows, (half + 1) * rows), slice(None))
         lanes = sums[kind].shape[3] // 2
@@ -720,7 +733,7 @@
             elif begin + value.shape[1] > target.shape[1]:
                 cut = target.shape[1] - begin
                 target[:, begin:] = value[:, :cut]
-                (out_bo if target is out_b else out_co)[...] = value[:, cut:]
+                out_bo[...] = value[:, cut:]
             else:
                 target[:, begin : begin + value.shape[1]] = value
         if step:
@@ -820,16 +833,21 @@
         in_specs=[vmem, vmem] + [hbm] * (1 + len(operands)),
         out_specs=(hbm,) + (vmem,) * 8,
         scratch_shapes=[
-            VMEM((6, clips, rows_w * frames, wide), bf16),
+            VMEM((5, clips, rows_w * frames, wide), bf16),
             VMEM((2, clips, rows_d * frames, narrow), bf16),
-            VMEM((6, clips // 2, rows_w * frames, wide), bf16),
+            VMEM((2, clips, rows_w * frames, width), bf16),
+            VMEM((5, clips // 2, rows_w * frames, wide), bf16),
             VMEM((2, clips // 2, rows_d * frames, narrow), bf16),
-            VMEM((6, 2, peers, rows_w * frames, wide // 2), bf16),
+            VMEM((2, clips // 2, rows_w * frames, width), bf16),
+            VMEM((5, 2, peers, rows_w * frames, wide // 2), bf16),
             VMEM((2, 2, peers, rows_d * frames // 2, narrow), bf16),
-            VMEM((6, frames, rows_w, wide), bf16),
+            VMEM((2, 2, peers, rows_w * frames, width // 2), bf16),
+            VMEM((5, frames, rows_w, wide), bf16),
             VMEM((2, frames, rows_d, narrow), bf16),
-            VMEM((6, frames - 1, rows_w, wide), bf16),
+            VMEM((2, frames, rows_w, width), bf16),
+            VMEM((5, frames - 1, rows_w, wide), bf16),
             VMEM((2, frames - 1, rows_d, narrow), bf16),
+            VMEM((2, frames - 1, rows_w, width), bf16),
             VMEM((SLOTS, STEP, width), bf16),
             VMEM((SLOTS, STEP, wide), bf16),
             VMEM((width, wide), f32),
@@ -837,9 +855,9 @@
             VMEM((frames,) + small.shape, f32),
             VMEM(small.shape, f32),
             DMA((SLOTS,)), DMA((SLOTS,)),
-            DMA((8, clips // 2)), DMA((8, clips // 2)),
-            DMA((8, 2, peers)), DMA((8, 2, peers)),
-            DMA((8, frames - 1)), DMA((8, frames - 1)),
+            DMA((9, clips // 2)), DMA((9, clips // 2)),
+            DMA((9, 2, peers)), DMA((9, 2, peers)),
+            DMA((9, frames - 1)), DMA((9, frames - 1)),
             DMA((frames - 1,)), DMA((frames - 1,)),
             DMA((clips - 1,)), DMA((clips - 1,)),
             DMA((clip_count * frame_count, frames - 1)),
@@ -1376,7 +1394,6 @@
     place = lax.broadcasted_iota(jnp.int32, (width, 128), 0) - owner * rows
     lane = lax.broadcasted_iota(jnp.int32, (width, 128), 1)
     select = ((place == lane) & (lane < rows)).astype(bf16)
-    ada = jnp.pad(ada_weight, ((0, 128 - rows), (0, 0)))
 
     def spread_bias(vector):
         length = vector.shape[0]
@@ -1392,14 +1409,12 @@
         ],
         axis=0,
     )
-    sh_c = jnp.concatenate([space_qkv, space_out], axis=1)
-    sh_b = jnp.concatenate([time_qkv, time_out], axis=1)
     (
         w_c, w_b, w_u, w_d, mod, chosen, totals, hidden_one, qkv_one, mixed_one, branch_one,
         after_first, after_later, cot_first,
     ) = start_call(
-        clips, frames, inputs, cotangent, sh_c, sh_b, up_weight, down_weight, embed, select, ada,
-        bias,
+        clips, frames, inputs, cotangent, space_qkv, space_out, time_qkv, time_out, up_weight,
+        down_weight, embed, select, ada_weight, bias,
     )
 
     def exchange(values):

time: 475 us -> 476 us (level)
  Pallas kernels: 428 us -> 435 us
where the time goes in v3:
time: 476 us; the launch traced here: 468 us
  Pallas kernels  435 us (91%)
  local copies, waits for them, and re-layouts  22.2 us (5%)
  other arithmetic  6.59 us (1%)
    pallas_call x1, Pallas kernels, middle_call(): pl.pallas_call(functools.partial(middle_kernel, clips, frames, tiles), gr...  136 us
    pallas_call x1, Pallas kernels, grad_call(): pl.pallas_call(functools.partial(grad_kernel, clips, frames, clip_count),...  131 us
    pallas_call x1, Pallas kernels, start_call(): pl.pallas_call(functools.partial(start_kernel, clips, frames, clip_count)...  123 us
    pallas_call x2, Pallas kernels, space_back_call(): pl.pallas_call(body, grid=(frame_count,), in_specs=in_specs, out_specs=[p...  44.6 us
    unnamed x26, local copies, waits for them, and re-layouts  9.72 us
  transfers between devices with their start and end apart: 1, of which 0 were waited for; matrix products, arithmetic and copies ran while one was open for 0% of the time, Pallas kernels for 5%

profile of v3, /device:TPU:0, one launch (start us, length us, event | category | flops | bytes accessed | tf_op | source)
XLA Modules:
  0.0 468.4 jit_solution(14194790627316354522)
XLA Ops:
  0.7 0.7 convert_element_type.29
  1.3 0.8 convert_dynamic-update-slice_fusion
  2.1 0.7 bitcast_convert_fusion.2
  2.8 0.7 bitcast_convert_fusion.1
  3.4 0.7 convert_dynamic-update-slice_fusion.1
  4.2 0.7 bitcast_convert_fusion
  4.9 0.7 multiply_exponential_fusion.1
  6.3 0.8 fusion.1.select
  7.6 2.0 concatenate.10.bias
  9.6 123.2 %shard_map.263 = (bf16[768,3072]{1,0:T(8,128)(2,1)}, bf16[768,3072]{1,0:T(8,128)(2,1)}, bf16[768,3072]{1,0:T(8,128)(2,1)}, bf16[3072,768]{1,0:T(8,128)(2,1)}, f3...) custom-call(bf16[2,4,256,768]{3,2,1,0:T(8,128)(2,1)} %refs_2_.1, ...), custom_call_target="tpu_custom_call" | custom-call | tf_op jit(solution)/shard_map/pallas_call | solution.py:450
  132.8 0.7 broadcast_in_dim.16.loss
  133.5 135.7 %shard_map.264 = (bf16[2048,3072]{1,0:T(8,128)(2,1)}, bf16[2048,3072]{1,0:T(8,128)(2,1)}, bf16[2048,768]{1,0:T(8,128)(2,1)}, bf16[2048,768]{1,0:T(8,128)(2,1)}, ...) custom-call(bf16[4,4,64,768]{3,2,1,0:T(8,128)(2,1)} %get-tuple-eleme, ...), custom_call_target="tpu_custom_call" | custom-call | tf_op jit(solution)/shard_map/pallas_call | solution.py:1250
  269.2 3.5 all-to-all-start
  272.8 22.3 %shard_map.265 = (f32[2,4,256,768]{3,2,1,0:T(8,128)}, bf16[2048,768]{1,0:T(8,128)(2,1)}, bf16[2048,2304]{1,0:T(8,128)(2,1)}, f32[8,768]{1,0:T(8,128)}) custom-call(bf16[4,4,64,768]{3,2,1,0:T(8,128)(2,1)} %get-tuple-element.65.refs_0_, bf16[2,4,256,768]{3,2,1,0:T(8,128)(2,1)} %refs_2_.1, f32[32,768]{1,0:T(8,128)} %get-tuple-element.61.mod.refs_2_.refs_3_, ...), custom_call_target="tpu_custom_call" | custom-call | flops 20480000000 | bytes 15728640 | tf_op jit(solution)/shard_map/pallas_call | solution.py:1356
  295.1 0.7 slice.61
  295.8 0.7 slice.77
  296.6 0.7 copy.34
  297.3 0.9 copy-done
  298.2 22.3 %shard_map.266 = (f32[2,4,256,768]{3,2,1,0:T(8,128)}, bf16[2048,768]{1,0:T(8,128)(2,1)}, bf16[2048,2304]{1,0:T(8,128)(2,1)}, f32[8,768]{1,0:T(8,128)}) custom-call(bf16[4,4,64,768]{3,2,1,0:T(8,128)(2,1)} %get-tuple-element.72.refs_0_, bf16[4,4,32,768]{3,2,1,0:T(8,128)(2,1)} %copy-done, ...), custom_call_target="tpu_custom_call", output_to_operand_aliasing={{0}: (8, {}), {1}: (9, {}), {2}: (10, {})} | custom-call | flops 20480000000 | bytes 15728640 | tf_op jit(solution)/shard_map/pallas_call | solution.py:1356
  320.6 0.7 slice.64
  321.3 0.8 slice_add_fusion
  322.4 0.6 pad.9.small
  323.1 131.4 %shard_map.267 = (bf16[2,4,256,768]{3,2,1,0:T(8,128)(2,1)}, f32[24,6912]{1,0:T(8,128)}, f32[16,768]{1,0:T(8,128)}, f32[24,3072]{1,0:T(8,128)}, f32[96,768]{1,0:T...) custom-call(f32[32,768]{1,0:T(8,128)} %pad.9.small, ...), custom_call_target="tpu_custom_call" | custom-call | tf_op jit(solution)/shard_map/pallas_call | solution.py:820
  454.5 0.9 fusion.6
  455.4 0.7 slice.75
  456.1 0.8 reshape.105
  459.4 3.9 copy.52
  463.2 0.8 copy.53
  464.1 0.7 copy.54
  465.4 0.7 copy.56
  466.7 0.7 copy.58
  467.5 0.7 copy.59
  (43 shorter events, 5.3 us)
Async XLA Ops:
  269.2 28.1 %all-to-all-start = ((bf16[4,4,32,768]{3,2,1,0:T(8,128)(2,1)}), bf16[4,4,32,768]{3,2,1,0:T(8,128)(2,1)S(1)}, u32[]{:S(2)}, u32[]{:S(2)}) async-start(bf16[4,4,32,768]{3,2,1,0:T(8,128)(2,1)} %get-tuple-element.73), calls=%async_computation | async-start | bytes 1572864 | tf_op jit(solution)/shard_map/all_to_all | solution.py:1421
  272.7 24.5 %copy-start.6 = (f32[2,16,768]{2,1,0:T(8,128)S(1)}, f32[2,16,768]{2,1,0:T(8,128)}, u32[]{:S(2)}) copy-start(f32[2,16,768]{2,1,0:T(8,128)} %get-tuple-element.71) | copy-start | bytes 294916
  297.3 0.9 copy-start
  459.3 3.9 copy-start.1
  459.3 4.8 %copy-start.5 = (f32[24,2304]{1,0:T(8,128)S(1)}, f32[24,2304]{1,0:T(8,128)}, u32[]{:S(2)}) copy-start(f32[24,2304]{1,0:T(8,128)} %get-tuple-element.130) | copy-start | bytes 663556
  459.3 5.5 %copy-start.8 = (f32[24,768]{1,0:T(8,128)S(1)}, f32[24,768]{1,0:T(8,128)}, u32[]{:S(2)}) copy-start(f32[24,768]{1,0:T(8,128)} %get-tuple-element.131) | copy-start | bytes 221188
  459.3 6.1 %copy-start.4 = (f32[24,2304]{1,0:T(8,128)S(1)}, f32[24,2304]{1,0:T(8,128)}, u32[]{:S(2)}) copy-start(f32[24,2304]{1,0:T(8,128)} %get-tuple-element.133) | copy-start | bytes 663556
  459.3 6.8 %copy-start.7 = (f32[24,768]{1,0:T(8,128)S(1)}, f32[24,768]{1,0:T(8,128)}, u32[]{:S(2)}) copy-start(f32[24,768]{1,0:T(8,128)} %get-tuple-element.134) | copy-start | bytes 221188
  459.3 7.4 %copy-start.3 = (f32[24,3072]{1,0:T(8,128)S(1)}, f32[24,3072]{1,0:T(8,128)}, u32[]{:S(2)}) copy-start(f32[24,3072]{1,0:T(8,128)} %get-tuple-element.136) | copy-start | bytes 884740
  459.4 8.1 %copy-start.2 = (f32[96,768]{1,0:T(8,128)S(1)}, f32[96,768]{1,0:T(8,128)}, u32[]{:S(2)}) copy-start(f32[96,768]{1,0:T(8,128)} %get-tuple-element.138) | copy-start | bytes 884740

commit v4 on v3

--- a/solution.py
+++ b/solution.py
@@ -504,8 +504,7 @@
     clips, frames, clip_count,
     small, chosen, out_all, h3, gup, act, gb3, h2, gqkv2, mix2, gb2, h1, gqkv1, mix1, gb1,
     outputs, grad_ada, bias_sums, out_u, out_d, out_b, out_bo, out_c, out_co,
-    sum_w, sum_d, sum_s, core_w, core_d, core_s, side_w, side_d, side_s,
-    line_w, line_d, line_s, last_w, last_d, last_s,
+    sum_w, sum_d, core_w, core_d, side_w, side_d, line_w, line_d, last_w, last_d,
     left, right, total, gathered, lined, held,
     lsem, rsem, cs, cr, xs, xr, zs, zr, fs, fr, ps, pr, os, orr, ks,
 ):
@@ -556,12 +555,10 @@
         (0, 2, [(h2, gqkv2, 0, 0, wide)], out_b, 0),
         (0, 3, [(h2, gqkv2, wide, 0, width), (mix2, gb2, 0, width, width)], out_b, wide),
         (0, 4, [(h1, gqkv1, 0, 0, wide)], out_c, 0),
-        (2, 0, [(h1, gqkv1, wide, 0, width)], out_c, wide),
-        (2, 1, [(mix1, gb1, 0, 0, width)], out_co, 0),
+        (0, 5, [(h1, gqkv1, wide, 0, width), (mix1, gb1, 0, width, width)], out_c, wide),
     ]
-    sums, cores = (sum_w, sum_d, sum_s), (core_w, core_d, core_s)
-    sides = (side_w, side_d, side_s)
-    lines, lasts = (line_w, line_d, line_s), (last_w, last_d, last_s)
+    sums, cores, sides = (sum_w, sum_d), (core_w, core_d), (side_w, side_d)
+    lines, lasts = (line_w, line_d), (last_w, last_d)
     flights = {}
 
     steps = tokens // STEP
@@ -646,7 +643,7 @@
         flights[number, "core"] = copies
 
     def half_of(kind, half):
-        if kind == 1:
+        if kind:
             rows = sums[kind].shape[2] // 2
             return (slice(half * rows, (half + 1) * rows), slice(None))
         lanes = sums[kind].shape[3] // 2
@@ -733,7 +730,7 @@
             elif begin + value.shape[1] > target.shape[1]:
                 cut = target.shape[1] - begin
                 target[:, begin:] = value[:, :cut]
-                out_bo[...] = value[:, cut:]
+                (out_bo if target is out_b else out_co)[...] = value[:, cut:]
             else:
                 target[:, begin : begin + value.shape[1]] = value
         if step:
@@ -833,21 +830,16 @@
         in_specs=[vmem, vmem] + [hbm] * (1 + len(operands)),
         out_specs=(hbm,) + (vmem,) * 8,
         scratch_shapes=[
-            VMEM((5, clips, rows_w * frames, wide), bf16),
+            VMEM((6, clips, rows_w * frames, wide), bf16),
             VMEM((2, clips, rows_d * frames, narrow), bf16),
-            VMEM((2, clips, rows_w * frames, width), bf16),
-            VMEM((5, clips // 2, rows_w * frames, wide), bf16),
+            VMEM((6, clips // 2, rows_w * frames, wide), bf16),
             VMEM((2, clips // 2, rows_d * frames, narrow), bf16),
-            VMEM((2, clips // 2, rows_w * frames, width), bf16),
-            VMEM((5, 2, peers, rows_w * frames, wide // 2), bf16),
+            VMEM((6, 2, peers, rows_w * frames, wide // 2), bf16),
             VMEM((2, 2, peers, rows_d * frames // 2, narrow), bf16),
-            VMEM((2, 2, peers, rows_w * frames, width // 2), bf16),
-            VMEM((5, frames, rows_w, wide), bf16),
+            VMEM((6, frames, rows_w, wide), bf16),
             VMEM((2, frames, rows_d, narrow), bf16),
-            VMEM((2, frames, rows_w, width), bf16),
-            VMEM((5, frames - 1, rows_w, wide), bf16),
+            VMEM((6, frames - 1, rows_w, wide), bf16),
             VMEM((2, frames - 1, rows_d, narrow), bf16),
-            VMEM((2, frames - 1, rows_w, width), bf16),
             VMEM((SLOTS, STEP, width), bf16),
             VMEM((SLOTS, STEP, wide), bf16),
             VMEM((width, wide), f32),
@@ -855,9 +847,9 @@
             VMEM((frames,) + small.shape, f32),
             VMEM(small.shape, f32),
             DMA((SLOTS,)), DMA((SLOTS,)),
-            DMA((9, clips // 2)), DMA((9, clips // 2)),
-            DMA((9, 2, peers)), DMA((9, 2, peers)),
-            DMA((9, frames - 1)), DMA((9, frames - 1)),
+            DMA((8, clips // 2)), DMA((8, clips // 2)),
+            DMA((8, 2, peers)), DMA((8, 2, peers)),
+            DMA((8, frames - 1)), DMA((8, frames - 1)),
             DMA((frames - 1,)), DMA((frames - 1,)),
             DMA((clips - 1,)), DMA((clips - 1,)),
             DMA((clip_count * frame_count, frames - 1)),

time: 476 us -> 472 us (level)
  no operation moved by 1% of the time
where the time goes in v4:
time: 472 us; the launch traced here: 464 us
  Pallas kernels  431 us (91%)
  local copies, waits for them, and re-layouts  22.2 us (5%)
  other arithmetic  6.59 us (1%)
    pallas_call x1, Pallas kernels, middle_call(): pl.pallas_call(functools.partial(middle_kernel, clips, frames, tiles), gr...  136 us
    pallas_call x1, Pallas kernels, grad_call(): pl.pallas_call(functools.partial(grad_kernel, clips, frames, clip_count),...  128 us
    pallas_call x1, Pallas kernels, start_call(): pl.pallas_call(functools.partial(start_kernel, clips, frames, clip_count)...  123 us
    pallas_call x2, Pallas kernels, space_back_call(): pl.pallas_call(body, grid=(frame_count,), in_specs=in_specs, out_specs=[p...  44.6 us
    unnamed x26, local copies, waits for them, and re-layouts  9.72 us
  transfers between devices with their start and end apart: 1, of which 0 were waited for; matrix products, arithmetic and copies ran while one was open for 0% of the time, Pallas kernels for 5%

profile of v4, /device:TPU:0, one launch (start us, length us, event | category | flops | bytes accessed | tf_op | source)
XLA Modules:
  0.0 464.5 jit_solution(298381857086058072)
XLA Ops:
  0.7 0.7 convert_element_type.29
  1.3 0.8 convert_dynamic-update-slice_fusion
  2.1 0.7 bitcast_convert_fusion.2
  2.8 0.7 bitcast_convert_fusion.1
  3.4 0.7 convert_dynamic-update-slice_fusion.1
  4.2 0.7 bitcast_convert_fusion
  4.9 0.7 multiply_exponential_fusion.1
  6.3 0.8 fusion.1.select
  7.6 2.0 concatenate.10.bias
  9.6 123.2 %shard_map.263 = (bf16[768,3072]{1,0:T(8,128)(2,1)}, bf16[768,3072]{1,0:T(8,128)(2,1)}, bf16[768,3072]{1,0:T(8,128)(2,1)}, bf16[3072,768]{1,0:T(8,128)(2,1)}, f3...) custom-call(bf16[2,4,256,768]{3,2,1,0:T(8,128)(2,1)} %refs_2_.1, ...), custom_call_target="tpu_custom_call" | custom-call | tf_op jit(solution)/shard_map/pallas_call | solution.py:450
  132.8 0.7 broadcast_in_dim.16.loss
  133.5 135.7 %shard_map.264 = (bf16[2048,3072]{1,0:T(8,128)(2,1)}, bf16[2048,3072]{1,0:T(8,128)(2,1)}, bf16[2048,768]{1,0:T(8,128)(2,1)}, bf16[2048,768]{1,0:T(8,128)(2,1)}, ...) custom-call(bf16[4,4,64,768]{3,2,1,0:T(8,128)(2,1)} %get-tuple-eleme, ...), custom_call_target="tpu_custom_call" | custom-call | tf_op jit(solution)/shard_map/pallas_call | solution.py:1242
  269.2 3.5 all-to-all-start
  272.8 22.3 %shard_map.265 = (f32[2,4,256,768]{3,2,1,0:T(8,128)}, bf16[2048,768]{1,0:T(8,128)(2,1)}, bf16[2048,2304]{1,0:T(8,128)(2,1)}, f32[8,768]{1,0:T(8,128)}) custom-call(bf16[4,4,64,768]{3,2,1,0:T(8,128)(2,1)} %get-tuple-element.65.refs_0_, bf16[2,4,256,768]{3,2,1,0:T(8,128)(2,1)} %refs_2_.1, f32[32,768]{1,0:T(8,128)} %get-tuple-element.61.mod.refs_2_.refs_3_, ...), custom_call_target="tpu_custom_call" | custom-call | flops 20480000000 | bytes 15728640 | tf_op jit(solution)/shard_map/pallas_call | solution.py:1348
  295.1 0.7 slice.61
  295.8 0.7 slice.77
  296.6 0.7 copy.34
  297.3 0.9 copy-done
  298.2 22.3 %shard_map.266 = (f32[2,4,256,768]{3,2,1,0:T(8,128)}, bf16[2048,768]{1,0:T(8,128)(2,1)}, bf16[2048,2304]{1,0:T(8,128)(2,1)}, f32[8,768]{1,0:T(8,128)}) custom-call(bf16[4,4,64,768]{3,2,1,0:T(8,128)(2,1)} %get-tuple-element.72.refs_0_, bf16[4,4,32,768]{3,2,1,0:T(8,128)(2,1)} %copy-done, ...), custom_call_target="tpu_custom_call", output_to_operand_aliasing={{0}: (8, {}), {1}: (9, {}), {2}: (10, {})} | custom-call | flops 20480000000 | bytes 15728640 | tf_op jit(solution)/shard_map/pallas_call | solution.py:1348
  320.6 0.7 slice.64
  321.3 0.8 slice_add_fusion
  322.4 0.6 pad.9.small
  323.1 127.5 %shard_map.267 = (bf16[2,4,256,768]{3,2,1,0:T(8,128)(2,1)}, f32[24,6912]{1,0:T(8,128)}, f32[16,768]{1,0:T(8,128)}, f32[24,3072]{1,0:T(8,128)}, f32[96,768]{1,0:T...) custom-call(f32[32,768]{1,0:T(8,128)} %pad.9.small, ...), custom_call_target="tpu_custom_call" | custom-call | tf_op jit(solution)/shard_map/pallas_call | solution.py:817
  450.6 0.9 fusion.6
  451.5 0.7 slice.75
  452.2 0.8 reshape.105
  455.4 3.9 copy.52
  459.3 0.8 copy.53
  460.2 0.7 copy.54
  461.5 0.7 copy.56
  462.8 0.7 copy.58
  463.5 0.7 copy.59
  (43 shorter events, 5.3 us)
Async XLA Ops:
  269.2 28.1 %all-to-all-start = ((bf16[4,4,32,768]{3,2,1,0:T(8,128)(2,1)}), bf16[4,4,32,768]{3,2,1,0:T(8,128)(2,1)S(1)}, u32[]{:S(2)}, u32[]{:S(2)}) async-start(bf16[4,4,32,768]{3,2,1,0:T(8,128)(2,1)} %get-tuple-element.73), calls=%async_computation | async-start | bytes 1572864 | tf_op jit(solution)/shard_map/all_to_all | solution.py:1413
  272.7 24.5 %copy-start.6 = (f32[2,16,768]{2,1,0:T(8,128)S(1)}, f32[2,16,768]{2,1,0:T(8,128)}, u32[]{:S(2)}) copy-start(f32[2,16,768]{2,1,0:T(8,128)} %get-tuple-element.71) | copy-start | bytes 294916
  297.3 0.9 copy-start
  455.4 3.9 copy-start.1
  455.4 4.8 %copy-start.5 = (f32[24,2304]{1,0:T(8,128)S(1)}, f32[24,2304]{1,0:T(8,128)}, u32[]{:S(2)}) copy-start(f32[24,2304]{1,0:T(8,128)} %get-tuple-element.130) | copy-start | bytes 663556
  455.4 5.5 %copy-start.8 = (f32[24,768]{1,0:T(8,128)S(1)}, f32[24,768]{1,0:T(8,128)}, u32[]{:S(2)}) copy-start(f32[24,768]{1,0:T(8,128)} %get-tuple-element.131) | copy-start | bytes 221188
  455.4 6.1 %copy-start.4 = (f32[24,2304]{1,0:T(8,128)S(1)}, f32[24,2304]{1,0:T(8,128)}, u32[]{:S(2)}) copy-start(f32[24,2304]{1,0:T(8,128)} %get-tuple-element.133) | copy-start | bytes 663556
  455.4 6.8 %copy-start.7 = (f32[24,768]{1,0:T(8,128)S(1)}, f32[24,768]{1,0:T(8,128)}, u32[]{:S(2)}) copy-start(f32[24,768]{1,0:T(8,128)} %get-tuple-element.134) | copy-start | bytes 221188
  455.4 7.4 %copy-start.3 = (f32[24,3072]{1,0:T(8,128)S(1)}, f32[24,3072]{1,0:T(8,128)}, u32[]{:S(2)}) copy-start(f32[24,3072]{1,0:T(8,128)} %get-tuple-element.136) | copy-start | bytes 884740
  455.4 8.1 %copy-start.2 = (f32[96,768]{1,0:T(8,128)S(1)}, f32[96,768]{1,0:T(8,128)}, u32[]{:S(2)}) copy-start(f32[96,768]{1,0:T(8,128)} %get-tuple-element.138) | copy-start | bytes 884740

commit v5 on v4

--- a/solution.py
+++ b/solution.py
@@ -1012,7 +1012,7 @@
         target = (after_tile, cot_tile)[number].at[place]
         return pltpu.make_async_copy(source.at[:, :, rows, :], target, ls.at[place, number])
 
-    early = tiles // 2
+    early = tiles // 4
 
     def grad_copies(index, later=False):
         place = index + tiles if later else index
@@ -1254,7 +1254,7 @@
             jax.ShapeDtypeStruct((2, 16, width), f32),
             traded, traded, traded, traded,
             jax.ShapeDtypeStruct(
-                (frames, frame_count, part - tiles // 2 * group, width), bf16
+                (frames, frame_count, part - tiles // 4 * group, width), bf16
             ),
             jax.ShapeDtypeStruct((2,) + after_first.shape, bf16),
         ],
@@ -1270,7 +1270,7 @@
             DMA((frames - 1,)), DMA((frames - 1,)),
             DMA((frames - 1,)), DMA((frames - 1,)),
             DMA((tiles, frames - 1)), DMA((tiles, frames - 1)),
-            DMA((max(tiles // 2, 1), frames - 1)), DMA((max(tiles // 2, 1), frames - 1)),
+            DMA((max(tiles // 4, 1), frames - 1)), DMA((max(tiles // 4, 1), frames - 1)),
             DMA((2, 2)), DMA((2,)), DMA((2, 2 * tiles)),
         ],
         compiler_params=pltpu.CompilerParams(

time: 472 us -> 473 us (level)
  transfers between devices with their start and end apart: 1 -> 1, of which waited for: 0 -> 1; matrix products, arithmetic and copies ran while one was open for 0% -> 0% of each run, Pallas kernels for 5% -> 5%
where the time goes in v5:
time: 473 us; the launch traced here: 465 us
  Pallas kernels  429 us (91%)
  local copies, waits for them, and re-layouts  22.3 us (5%)
  other arithmetic  6.59 us (1%)
    pallas_call x1, Pallas kernels, middle_call(): pl.pallas_call(functools.partial(middle_kernel, clips, frames, tiles), gr...  136 us
    pallas_call x1, Pallas kernels, grad_call(): pl.pallas_call(functools.partial(grad_kernel, clips, frames, clip_count),...  126 us
    pallas_call x1, Pallas kernels, start_call(): pl.pallas_call(functools.partial(start_kernel, clips, frames, clip_count)...  123 us
    pallas_call x2, Pallas kernels, space_back_call(): pl.pallas_call(body, grid=(frame_count,), in_specs=in_specs, out_specs=[p...  44.6 us
    unnamed x26, local copies, waits for them, and re-layouts  9.84 us
  transfers between devices with their start and end apart: 1, of which 1 were waited for; matrix products, arithmetic and copies ran while one was open for 0% of the time, Pallas kernels for 5%

profile of v5, /device:TPU:0, one launch (start us, length us, event | category | flops | bytes accessed | tf_op | source)
XLA Modules:
  0.0 465.3 jit_solution(15423754633105942007)
XLA Ops:
  0.7 0.7 convert_element_type.29
  1.3 0.8 convert_dynamic-update-slice_fusion
  2.1 0.7 bitcast_convert_fusion.2
  2.8 0.7 bitcast_convert_fusion.1
  3.4 0.7 convert_dynamic-update-slice_fusion.1
  4.2 0.7 bitcast_convert_fusion
  4.9 0.7 multiply_exponential_fusion.1
  6.3 0.8 fusion.1.select
  7.6 2.0 concatenate.10.bias
  9.6 123.2 %shard_map.263 = (bf16[768,3072]{1,0:T(8,128)(2,1)}, bf16[768,3072]{1,0:T(8,128)(2,1)}, bf16[768,3072]{1,0:T(8,128)(2,1)}, bf16[3072,768]{1,0:T(8,128)(2,1)}, f3...) custom-call(bf16[2,4,256,768]{3,2,1,0:T(8,128)(2,1)} %refs_2_.1, ...), custom_call_target="tpu_custom_call" | custom-call | tf_op jit(solution)/shard_map/pallas_call | solution.py:450
  132.8 0.7 broadcast_in_dim.16.loss
  133.5 135.6 %shard_map.264 = (bf16[2048,3072]{1,0:T(8,128)(2,1)}, bf16[2048,3072]{1,0:T(8,128)(2,1)}, bf16[2048,768]{1,0:T(8,128)(2,1)}, bf16[2048,768]{1,0:T(8,128)(2,1)}, ...) custom-call(bf16[4,4,64,768]{3,2,1,0:T(8,128)(2,1)} %get-tuple-eleme, ...), custom_call_target="tpu_custom_call" | custom-call | tf_op jit(solution)/shard_map/pallas_call | solution.py:1242
  269.1 3.5 all-to-all-start
  272.6 22.3 %shard_map.265 = (f32[2,4,256,768]{3,2,1,0:T(8,128)}, bf16[2048,768]{1,0:T(8,128)(2,1)}, bf16[2048,2304]{1,0:T(8,128)(2,1)}, f32[8,768]{1,0:T(8,128)}) custom-call(bf16[4,4,64,768]{3,2,1,0:T(8,128)(2,1)} %get-tuple-element.65.refs_0_, bf16[2,4,256,768]{3,2,1,0:T(8,128)(2,1)} %refs_2_.1, f32[32,768]{1,0:T(8,128)} %get-tuple-element.61.mod.refs_2_.refs_3_, ...), custom_call_target="tpu_custom_call" | custom-call | flops 20480000000 | bytes 15728640 | tf_op jit(solution)/shard_map/pallas_call | solution.py:1348
  295.0 0.7 slice.61
  295.7 0.7 slice.77
  296.5 0.7 copy.34
  297.2 2.5 all-to-all-done.refs_1_
  299.7 1.0 copy-done
  300.7 22.2 %shard_map.266 = (f32[2,4,256,768]{3,2,1,0:T(8,128)}, bf16[2048,768]{1,0:T(8,128)(2,1)}, bf16[2048,2304]{1,0:T(8,128)(2,1)}, f32[8,768]{1,0:T(8,128)}) custom-call(bf16[4,4,64,768]{3,2,1,0:T(8,128)(2,1)} %get-tuple-element.72.refs_0_, bf16[4,4,48,768]{3,2,1,0:T(8,128)(2,1)} %copy-done, ...), custom_call_target="tpu_custom_call", output_to_operand_aliasing={{0}: (8, {}), {1}: (9, {}), {2}: (10, {})} | custom-call | flops 20480000000 | bytes 15728640 | tf_op jit(solution)/shard_map/pallas_call | solution.py:1348
  323.0 0.7 slice.64
  323.7 0.8 slice_add_fusion
  325.5 125.9 %shard_map.267 = (bf16[2,4,256,768]{3,2,1,0:T(8,128)(2,1)}, f32[24,6912]{1,0:T(8,128)}, f32[16,768]{1,0:T(8,128)}, f32[24,3072]{1,0:T(8,128)}, f32[96,768]{1,0:T...) custom-call(f32[32,768]{1,0:T(8,128)} %pad.9.small, ...), custom_call_target="tpu_custom_call" | custom-call | tf_op jit(solution)/shard_map/pallas_call | solution.py:817
  451.4 0.9 fusion.6
  452.3 0.7 slice.75
  453.0 0.8 reshape.105
  456.2 3.9 copy.52
  460.1 0.8 copy.53
  461.0 0.7 copy.54
  462.3 0.7 copy.56
  463.6 0.7 copy.58
  464.3 0.7 copy.59
  (43 shorter events, 5.9 us)
Async XLA Ops:
  269.1 30.6 %all-to-all-start = ((bf16[4,4,48,768]{3,2,1,0:T(8,128)(2,1)}), bf16[4,4,48,768]{3,2,1,0:T(8,128)(2,1)S(1)}, u32[]{:S(2)}, u32[]{:S(2)}) async-start(bf16[4,4,48,768]{3,2,1,0:T(8,128)(2,1)} %get-tuple-element.73), calls=%async_computation | async-start | bytes 2359296 | tf_op jit(solution)/shard_map/all_to_all | solution.py:1413
  272.6 24.6 %copy-start.6 = (f32[2,16,768]{2,1,0:T(8,128)S(1)}, f32[2,16,768]{2,1,0:T(8,128)}, u32[]{:S(2)}) copy-start(f32[2,16,768]{2,1,0:T(8,128)} %get-tuple-element.71) | copy-start | bytes 294916
  299.7 1.0 copy-start
  456.2 3.9 copy-start.1
  456.2 4.8 %copy-start.5 = (f32[24,2304]{1,0:T(8,128)S(1)}, f32[24,2304]{1,0:T(8,128)}, u32[]{:S(2)}) copy-start(f32[24,2304]{1,0:T(8,128)} %get-tuple-element.130) | copy-start | bytes 663556
  456.2 5.5 %copy-start.8 = (f32[24,768]{1,0:T(8,128)S(1)}, f32[24,768]{1,0:T(8,128)}, u32[]{:S(2)}) copy-start(f32[24,768]{1,0:T(8,128)} %get-tuple-element.131) | copy-start | bytes 221188
  456.2 6.1 %copy-start.4 = (f32[24,2304]{1,0:T(8,128)S(1)}, f32[24,2304]{1,0:T(8,128)}, u32[]{:S(2)}) copy-start(f32[24,2304]{1,0:T(8,128)} %get-tuple-element.133) | copy-start | bytes 663556
  456.2 6.8 %copy-start.7 = (f32[24,768]{1,0:T(8,128)S(1)}, f32[24,768]{1,0:T(8,128)}, u32[]{:S(2)}) copy-start(f32[24,768]{1,0:T(8,128)} %get-tuple-element.134) | copy-start | bytes 221188
  456.2 7.4 %copy-start.3 = (f32[24,3072]{1,0:T(8,128)S(1)}, f32[24,3072]{1,0:T(8,128)}, u32[]{:S(2)}) copy-start(f32[24,3072]{1,0:T(8,128)} %get-tuple-element.136) | copy-start | bytes 884740
  456.2 8.1 %copy-start.2 = (f32[96,768]{1,0:T(8,128)S(1)}, f32[96,768]{1,0:T(8,128)}, u32[]{:S(2)}) copy-start(f32[96,768]{1,0:T(8,128)} %get-tuple-element.138) | copy-start | bytes 884740
